TPU v7x, 128 devices: a whole 4x4x4 slice. The times are simulated.
128 devices in a mesh: dp: 2 (over z_hi), expert: 8 (over y, core), tensor: 8 (over z_lo, x).
Axes of the slice: x: 4, y: 4, z: 4 (z_hi: 2, z_lo: 2; z = z_hi * 2 + z_lo), core: 2. Of those that a mesh axis runs over, the one named last changes fastest.
Arguments:
- tokens: bfloat16 [2048, 3072], P(('dp', 'expert')), may hold values from -6 to 6
- cotangent: bfloat16 [2048, 3072], P(('dp', 'expert', 'tensor')), may hold values from -6 to 6
- expert_ids: int32 [2048, 2], P(('dp', 'expert')), may hold values from 0 to 7, all different within a row; in each aligned block of 128 rows (0 to 127, 128 to 255, ...) at most 36 rows name the same one
- route_weight: float32 [2048, 2], P(('dp', 'expert')), may hold values from 0.1 to 1
- w_up: bfloat16 [8, 3072, 16384], P('expert', 'dp', 'tensor'), may hold values from -0.109375 to 0.109375
- w_down: bfloat16 [8, 3072, 16384], P('expert', 'dp', 'tensor'), may hold values from -0.046875 to 0.046875
Outputs:
- input_grad: bfloat16 [2048, 3072], P(('dp', 'expert', 'tensor'))
- grad_up: bfloat16 [8, 3072, 16384], P('expert', 'dp', 'tensor')
- grad_down: bfloat16 [8, 3072, 16384], P('expert', 'dp', 'tensor')
Inputs may be any that keep to these rules, and one draw needn't show every extreme that they name: `expert_ids`: the 2 ids of a token differ. Among the ids of the 128 tokens of one group (aligned blocks of 128 rows) no expert is named more than 36 times, a bound that some block reaches.
All inputs are finite; a program needn't handle non-finite values.
Results may differ from a plain program's by a relative error of at most 0.0057.
Values may be sent and summed in bfloat16 or wider, within the bound.
A program may use at most 128 MiB of HBM per device.

v0:
```python
import jax
import jax.numpy as jnp
from jax import lax
from jax.sharding import PartitionSpec as P


def contract_rows(left, right):
    return lax.dot_general(
        left, right, (((0,), (0,)), ((), ())), preferred_element_type=jnp.float32
    )


def contract_cols(left, right):
    return lax.dot_general(
        left, right, (((1,), (1,)), ((), ())), preferred_element_type=jnp.float32
    )


def activate(up_val, d_act):
    sigma = jax.nn.sigmoid(up_val)
    act = (up_val * sigma).astype(jnp.bfloat16)
    d_up = (d_act * sigma * (1.0 + up_val * (1.0 - sigma))).astype(jnp.bfloat16)
    return (act, d_up)


def shards(tokens, cotangent, expert_ids, route_weight, w_up, w_down):
    n_expert = lax.axis_size("expert")
    n_dp = lax.axis_size("dp")
    experts = w_up.shape[0] * n_expert
    group_rows = tokens.shape[0]
    width = tokens.shape[1]
    routes = expert_ids.shape[1]
    capacity = 9 * group_rows * routes // (8 * experts)
    half_width = w_up.shape[1]
    full_cot = lax.all_gather(cotangent, "tensor", axis=0, tiled=True)
    flat_ids = expert_ids.reshape(-1)
    hot = (flat_ids[:, None] == jnp.arange(experts, dtype=jnp.int32)[None, :]).astype(jnp.int32)
    before = jnp.cumsum(hot, axis=0) - hot
    slot = jnp.sum(before * hot, axis=1)
    target = flat_ids * capacity + slot
    placing = (jnp.arange(experts * capacity, dtype=jnp.int32)[:, None] == target[None, :]).astype(
        jnp.bfloat16
    )
    rows_x = jnp.repeat(tokens, routes, axis=0)
    rows_c = jnp.repeat(full_cot, routes, axis=0).astype(jnp.float32)
    scaled = (route_weight.reshape(-1)[:, None] * rows_c).astype(jnp.bfloat16)
    send_x = (
        jnp.dot(placing, rows_x, preferred_element_type=jnp.float32)
        .astype(jnp.bfloat16)
        .reshape(1, experts, capacity, width)
    )
    send_d = (
        jnp.dot(placing, scaled, preferred_element_type=jnp.float32)
        .astype(jnp.bfloat16)
        .reshape(1, experts, capacity, width)
    )
    recv_x, recv_d = (
        lax.all_to_all(send_x, "expert", split_axis=1, concat_axis=1, tiled=True),
        lax.all_to_all(send_d, "expert", split_axis=1, concat_axis=1, tiled=True),
    )
    got_x, got_d = (
        lax.all_to_all(recv_x, "dp", split_axis=3, concat_axis=0, tiled=True),
        lax.all_to_all(recv_d, "dp", split_axis=3, concat_axis=0, tiled=True),
    )
    all_x = got_x.reshape(-1, half_width)
    all_d = got_d.reshape(-1, half_width)
    up_w = w_up[0]
    down_w = w_down[0]
    up_part = jnp.dot(all_x, up_w, preferred_element_type=jnp.float32)
    dact_part = jnp.dot(all_d, down_w, preferred_element_type=jnp.float32)
    up_sum, dact_sum = lax.psum((up_part, dact_part), "dp")
    act, d_up = activate(up_sum, dact_sum)
    grad_u = contract_rows(all_x, d_up).astype(jnp.bfloat16)[None]
    grad_d = contract_rows(all_d, act).astype(jnp.bfloat16)[None]
    route_part = contract_cols(d_up, up_w).reshape(n_dp, n_expert, capacity, half_width)
    middle = lax.all_to_all(route_part, "expert", split_axis=1, concat_axis=1, tiled=True)
    back = lax.all_to_all(middle, "dp", split_axis=0, concat_axis=3, tiled=True)
    slot_rows = back.reshape(experts * capacity, width)
    picked = slot_rows[target]
    token_part = jnp.sum(picked.reshape(group_rows, routes, width), axis=1)
    summed = lax.psum_scatter(token_part, "tensor", scatter_dimension=0, tiled=True)
    return (summed.astype(jnp.bfloat16), grad_u, grad_d)


def solution(mesh):
    placed = (
        P(("dp", "expert"), None),
        P(("dp", "expert", "tensor"), None),
        P(("dp", "expert"), None),
        P(("dp", "expert"), None),
        P("expert", "dp", "tensor"),
        P("expert", "dp", "tensor"),
    )
    return jax.shard_map(
        shards,
        mesh=mesh,
        in_specs=placed,
        out_specs=(
            P(("dp", "expert", "tensor"), None),
            P("expert", "dp", "tensor"),
            P("expert", "dp", "tensor"),
        ),
        check_vma=False,
    )
```

profile of v0, /device:TPU:9, one launch (start us, length us, event | category | flops | bytes accessed | tf_op | source)
XLA Modules:
  0.0 633.9 jit_solution(4959144268512609733)
XLA Ops:
  9.2 25.3 %all_gather.3 = bf16[128,3072]{1,0:T(8,128)(2,1)S(1)} all-gather(bf16[16,3072]{1,0:T(8,128)(2,1)} %param.7), channel_id=1, replica_groups=mesh['dp'=2,'expert'=8,'tensor'=8] {'tensor'}, dimensions={0}, use_global_device_ids=true | all-gather | bytes 884736 | tf_op jit(solution)/shard_map/all_gather | solution.py:35
  43.0 10.7 %all-to-all-start = ((bf16[1,8,36,3072]{3,2,0,1:T(8,128)(2,1)}), bf16[1,8,36,3072]{3,2,0,1:T(8,128)(2,1)}, u32[]{:S(2)}, u32[]{:S(2)}) async-start(bf16[1,8,36,3072]{3,2,0,1:T(8,128)(2,1)} %bitcast.61), calls=%async_computation | async-start | bytes 3932160 | tf_op jit(solution)/shard_map/all_to_all | solution.py:59
  57.2 20.4 %all-to-all-done = bf16[1,8,36,3072]{3,2,0,1:T(8,128)(2,1)} async-done(((bf16[1,8,36,3072]{3,2,0,1:T(8,128)(2,1)}), bf16[1,8,36,3072]{3,2,0,1:T(8,128)(2,1)}, u32[]{:S(2)}, u32[]{:S(2)}) %all-to-all-start) | async-done | bytes 1769504 | tf_op jit(solution)/shard_map/all_to_all | solution.py:59
  77.6 5.7 all-to-all-start.2
  83.2 7.6 %copy.22 = bf16[1,8,36,3072]{2,1,0,3:T(8,128)(2,1)} copy(bf16[1,8,36,3072]{3,2,0,1:T(8,128)(2,1)} %all-to-all-done) | data formatting | bytes 3538944 | tf_op jit(solution)/shard_map/all_to_all | solution.py:59
  90.8 18.6 %reshape.112 = bf16[2,2,221184]{2,1,0:T(2,128)(2,1)} reshape(bf16[3072,1,8,36]{3,2,1,0:T(8,128)(2,1)} %bitcast.54) | data formatting | bytes 3538944
  109.4 4.9 all-to-all-start.1
  114.3 5.9 copy.26
  120.3 18.6 %reshape.110 = bf16[2,2,221184]{2,1,0:T(2,128)(2,1)} reshape(bf16[3072,1,8,36]{3,2,1,0:T(8,128)(2,1)} %bitcast.55) | data formatting | bytes 3538944
  138.9 4.7 all-to-all-start.3
  144.0 19.9 %reshape.113 = bf16[3072,1,8,36]{3,2,1,0:T(8,128)(2,1)} reshape(bf16[2,2,221184]{2,1,0:T(2,128)(2,1)} %all-to-all-done.1) | data formatting | bytes 3538944
  163.9 10.6 %copy.34 = bf16[1,8,36,2,1536]{4,3,1,2,0:T(2,128)(2,1)} copy(bf16[1,8,36,2,1536]{2,1,4,3,0:T(8,128)(2,1)} %bitcast.56) | data formatting | bytes 3538944 | tf_op jit(solution)/shard_map/all_to_all | solution.py:63
  178.4 19.9 %reshape.111 = bf16[3072,1,8,36]{3,2,1,0:T(8,128)(2,1)} reshape(bf16[2,2,221184]{2,1,0:T(2,128)(2,1)} %all-to-all-done.3) | data formatting | bytes 3538944
  198.3 10.7 %copy.35 = bf16[1,8,36,2,1536]{4,3,1,2,0:T(2,128)(2,1)} copy(bf16[1,8,36,2,1536]{2,1,4,3,0:T(8,128)(2,1)} %bitcast.57) | data formatting | bytes 3538944 | tf_op jit(solution)/shard_map/all_to_all | solution.py:62
  212.9 9.4 %fusion.6 = f32[576,2048]{1,0:T(8,128)} fusion(bf16[576,1536]{1,0:T(8,128)(2,1)} %reshape.94, bf16[1,1536,2048]{2,1,0:T(8,128)(2,1)} %param.11), kind=kOutput, calls=%fused_computation.9 | convolution fusion | flops 3623878656 | bytes 12779520 | tf_op jit(solution)/shard_map/dot_general | solution.py:70
  222.3 8.4 %fusion.4 = f32[576,2048]{1,0:T(8,128)} fusion(bf16[576,1536]{1,0:T(8,128)(2,1)S(1)} %copy-done.2, bf16[1,1536,2048]{2,1,0:T(8,128)(2,1)} %param.10), kind=kOutput, calls=%fused_computation.7 | convolution fusion | flops 3623878656 | bytes 12779520 | tf_op jit(solution)/shard_map/dot_general | solution.py:69
  230.7 230.9 %all-reduce.3.cloned.1.call-done = (f32[576,2048]{1,0:T(8,128)}, f32[576,2048]{1,0:T(8,128)}) async-done(((f32[576,2048]{1,0:T(8,128)}, f32[576,2048]{1,0:T(8,128)}), (f32[576,2048]{1,0:T(8,128)}, f32[576,2048]{1,0:T(8,128)})) %all-reduce.3.cloned.1.call-update) | async-done | bytes 9437200 | tf_op jit(solution)/shard_map/psum | solution.py:71
  468.8 7.2 %fusion.2 = f32[2,8,36,1536]{3,2,1,0:T(8,128)S(1)} fusion(bf16[2,8,36,2048]{3,2,1,0:T(8,128)(2,1)} %dot_general.27, bf16[1,1536,2048]{2,1,0:T(8,128)(2,1)} %param.10), kind=kOutput, calls=%fused_computation.5 | convolution fusion | flops 3623878656 | bytes 12189696 | tf_op jit(solution)/shard_map/dot_general | solution.py:14
  478.8 46.4 %all_to_all.60 = f32[2,8,36,1536]{3,0,2,1:T(2,128)S(1)} all-to-all(f32[2,8,36,1536]{3,0,2,1:T(2,128)S(1)} %copy.29), channel_id=1, replica_groups=mesh['dp'=2,'expert'=8,'tensor'=8] {'expert'}, dimensions={1} | all-to-all | bytes 7077888 | tf_op jit(solution)/shard_map/all_to_all | solution.py:76
  535.0 39.1 %all-to-all-done.5 = f32[2,8,36,1536]{3,1,2,0:T(8,128)S(1)} async-done(((f32[2,8,36,1536]{3,1,2,0:T(8,128)}), f32[2,8,36,1536]{3,1,2,0:T(8,128)S(1)}, u32[]{:S(2)}, u32[]{:S(2)}) %all-to-all-start.5) | async-done | bytes 3538976 | tf_op jit(solution)/shard_map/all_to_all | solution.py:77
  584.8 5.4 reduce_sum.22
  590.3 9.0 %fusion = bf16[1,1536,2048]{2,1,0:T(8,128)(2,1)} fusion(bf16[576,1536]{1,0:T(8,128)(2,1)} %reshape.97, bf16[576,2048]{1,0:T(8,128)(2,1)} %copy-done), kind=kOutput, calls=%fused_computation.3 | convolution fusion | flops 3627024384 | bytes 10420224 | tf_op jit(solution)/shard_map/dot_general | solution.py:8
  599.2 7.2 %fusion.1 = bf16[1,1536,2048]{2,1,0:T(8,128)(2,1)} fusion(bf16[576,1536]{1,0:T(8,128)(2,1)S(1)} %copy-done.1, f32[576,2048]{1,0:T(8,128)S(1)} %bitcast.65), kind=kOutput, calls=%fused_computation.4 | convolution fusion | flops 3632922624 | bytes 12779520 | tf_op jit(solution)/shard_map/dot_general | solution.py:8
  606.5 18.7 %reduce-scatter.2.cloned.1.call-done = f32[16,3072]{1,0:T(8,128)} async-done(((f32[128,3072]{1,0:T(8,128)}), f32[16,3072]{1,0:T(8,128)}) %reduce-scatter.2.cloned.1.call-update) | async-done | bytes 196624 | tf_op jit(solution)/shard_map/reduce_scatter | solution.py:81
  (63 shorter events, 54.2 us)
Async XLA Ops:
  35.3 3.3 copy-start.5
  41.5 12.1 %copy-start.3 = (bf16[128,3072]{1,0:T(8,128)(2,1)S(1)}, bf16[128,3072]{1,0:T(8,128)(2,1)}, u32[]{:S(2)}) copy-start(bf16[128,3072]{1,0:T(8,128)(2,1)} %param.6) | copy-start | bytes 2359300
  43.0 34.6 %all-to-all-start = ((bf16[1,8,36,3072]{3,2,0,1:T(8,128)(2,1)}), bf16[1,8,36,3072]{3,2,0,1:T(8,128)(2,1)}, u32[]{:S(2)}, u32[]{:S(2)}) async-start(bf16[1,8,36,3072]{3,2,0,1:T(8,128)(2,1)} %bitcast.61), calls=%async_computation | async-start | bytes 3932160 | tf_op jit(solution)/shard_map/all_to_all | solution.py:59
  77.6 31.9 %all-to-all-start.2 = ((bf16[1,8,36,3072]{3,2,0,1:T(8,128)(2,1)}), bf16[1,8,36,3072]{3,2,0,1:T(8,128)(2,1)S(1)}, u32[]{:S(2)}, u32[]{:S(2)}) async-start(bf16[1,8,36,3072]{3,2,0,1:T(8,128)(2,1)} %bitcast.60), calls=%async_computation.2 | async-start | bytes 3932160 | tf_op jit(solution)/shard_map/all_to_all | solution.py:58
  109.4 29.4 %all-to-all-start.1 = ((bf16[2,2,221184]{2,1,0:T(2,128)(2,1)}), bf16[2,2,221184]{2,1,0:T(2,128)(2,1)}, u32[]{:S(2)}, u32[]{:S(2)}) async-start(bf16[2,2,221184]{2,1,0:T(2,128)(2,1)} %reshape.112), calls=%async_computation.1 | async-start | bytes 3538944 | tf_op jit(solution)/shard_map/all_to_all | solution.py:63
  138.9 39.5 %all-to-all-start.3 = ((bf16[2,2,221184]{2,1,0:T(2,128)(2,1)}), bf16[2,2,221184]{2,1,0:T(2,128)(2,1)}, u32[]{:S(2)}, u32[]{:S(2)}) async-start(bf16[2,2,221184]{2,1,0:T(2,128)(2,1)} %reshape.110), calls=%async_computation.3 | async-start | bytes 3538944 | tf_op jit(solution)/shard_map/all_to_all | solution.py:62
  143.6 318.0 %all-reduce.3.cloned.1.call-start = ((), (), s32[]{:S(2)}) async-start(), calls=%async_computation.8 | async-start | bytes 18874368 | tf_op jit(solution)/shard_map/psum | solution.py:71
  212.9 9.5 %copy-start.2 = (bf16[576,1536]{1,0:T(8,128)(2,1)S(1)}, bf16[576,1536]{1,0:T(8,128)(2,1)}, u32[]{:S(2)}) copy-start(bf16[576,1536]{1,0:T(8,128)(2,1)} %reshape.97) | copy-start | bytes 5308420
  466.2 9.8 %copy-start = (bf16[576,2048]{1,0:T(8,128)(2,1)}, bf16[576,2048]{1,0:T(8,128)(2,1)S(1)}, u32[]{:S(2)}) copy-start(bf16[576,2048]{1,0:T(8,128)(2,1)S(1)} %multiply_convert_fusion.1) | copy-start | bytes 7077892
  529.0 4.2 copy-start.4
  529.0 45.1 %all-to-all-start.5 = ((f32[2,8,36,1536]{3,1,2,0:T(8,128)}), f32[2,8,36,1536]{3,1,2,0:T(8,128)S(1)}, u32[]{:S(2)}, u32[]{:S(2)}) async-start(f32[2,8,36,1536]{3,1,2,0:T(8,128)} %copy.30), calls=%async_computation.5 | async-start | bytes 7077888 | tf_op jit(solution)/shard_map/all_to_all | solution.py:77
  533.2 92.0 %reduce-scatter.2.cloned.1.call-start = ((), (), s32[]{:S(2)}) async-start(), calls=%async_computation.7 | async-start | bytes 1769472 | tf_op jit(solution)/shard_map/reduce_scatter | solution.py:81
  590.2 9.0 %slice-start = ((s8[4718592]{0:T(1024)(128)(4,1)}), s8[524288]{0:T(1024)(128)(4,1)S(1)}, s32[]{:S(2)}) async-start(s8[4718592]{0:T(1024)(128)(4,1)} %bitcast.64), calls=%async_computation.9 | async-start | bytes 1048576
  590.2 9.0 %slice-start.1 = ((s8[4718592]{0:T(1024)(128)(4,1)}), s8[4194304]{0:T(1024)(128)(4,1)S(1)}, s32[]{:S(2)}) async-start(s8[4718592]{0:T(1024)(128)(4,1)} %bitcast.64), calls=%async_computation.10 | async-start | bytes 8388608
  590.3 9.0 %copy-start.1 = (bf16[576,1536]{1,0:T(8,128)(2,1)S(1)}, bf16[576,1536]{1,0:T(8,128)(2,1)}, u32[]{:S(2)}) copy-start(bf16[576,1536]{1,0:T(8,128)(2,1)} %reshape.94) | copy-start | bytes 5308420
Sparse Core Ops, SparseCore 0:
  230.8 230.7 all-reduce.2
  590.4 34.7 reduce-scatter.1
where the time goes:
time: 645 us; the launch traced here: 634 us
  waiting for transfers between devices  309 us (48%)
  local copies, waits for them, and re-layouts  151 us (23%)
  blocking collectives  71.6 us (11%)
  matrix products  44.5 us (7%)
  starting transfers between devices  30.6 us (5%)
  between operations  14.6 us (2%)
  other arithmetic  12.3 us (2%)
    psum x1, waiting for transfers between devices, shards(): up_sum, dact_sum = lax.psum((up_part, dact_part), 'dp')  231 us
    unnamed x23, local copies, waits for them, and re-layouts  78.6 us
    all_to_all x1, blocking collectives, shards(): lax.all_to_all(route_part, 'expert', split_axis=1, concat_axis=1, tiled=T...  46.4 us
    all_to_all x1, waiting for transfers between devices, shards(): back = lax.all_to_all(middle, 'dp', split_axis=0, concat_axis=3, tiled=True)  39.1 us
    all_gather x1, blocking collectives, shards(): full_cot = lax.all_gather(cotangent, 'tensor', axis=0, tiled=True)  25.3 us
    all_to_all x1, waiting for transfers between devices, shards(): lax.all_to_all(send_d, 'expert', split_axis=1, concat_axis=1, tiled=True)  20.4 us
    reduce_scatter x1, waiting for transfers between devices, shards(): lax.psum_scatter(token_part, 'tensor', scatter_dimension=0, tiled=True)  18.7 us
    dot_general x2, matrix products, contract_rows(): lax.dot_general(left, right, (((0,), (0,)), ((), ())), preferred_element_...  16.2 us
  transfers between devices with their start and end apart: 7, of which 4 were waited for; matrix products, arithmetic and copies ran while one was open for 17% of the time, Pallas kernels for 0%

commit v1 on v0

v1 whole, which is shorter than its diff:
```python
import jax
import jax.numpy as jnp
from jax import lax
from jax.experimental import pallas as pl
from jax.experimental.pallas import tpu as pltpu
from jax.sharding import PartitionSpec as P

CAP = 36
GRP = 128
RC = 4 * CAP
TOKC = 4 * GRP
NF = 4
MESH = pl.DeviceIdType.MESH
BF = jnp.bfloat16
F32 = jnp.float32


def kernel(
    tok,
    cot,
    ids,
    rw,
    wu_hbm,
    wd_hbm,
    out,
    xd_hbm,
    ad_hbm,
    w,
    gat,
    metas,
    slotcol,
    rwcol,
    stage,
    xd,
    own,
    zs,
    zr,
    ad,
    acc,
    c1s,
    c1r,
    c2s,
    res,
    fin_s,
    fin_r,
    w_sem,
    cot_ss,
    cot_rs,
    tok_ss,
    tok_rs,
    met_ss,
    met_rs,
    d_ss,
    d_rs,
    z_ss,
    z_rs,
    c1_ss,
    c1_rs,
    c2_ss,
    c2_rs,
    f_ss,
    f_rs,
    o_sem,
    x_sem,
):
    dp, e, t = lax.axis_index("dp"), lax.axis_index("expert"), lax.axis_index("tensor")
    y, c = e // 2, e % 2
    zlo, x = t // 4, t % 4
    half = w.shape[2]
    fc = w.shape[3]
    xb_w = half // 4

    def at(src, dst, ss, rs, dev):
        return pltpu.make_async_remote_copy(
            src_ref=src, dst_ref=dst, send_sem=ss, recv_sem=rs, device_id=dev, device_id_type=MESH
        )

    def loop(lo, hi, fn):
        def step(i, carry):
            fn(i)
            return carry

        lax.fori_loop(lo, hi, step, 0)

    def w_copy(m, f):
        src = wu_hbm if m == 0 else wd_hbm
        return pltpu.make_async_copy(
            src.at[0, :, pl.ds(pl.multiple_of(f * fc, fc), fc)], w.at[m, f], w_sem.at[m, f]
        )

    for m in range(2):
        for f in range(NF):
            w_copy(m, f).start()

    barrier = pltpu.get_barrier_semaphore()
    me32 = (dp * 8 + t) * 2 + c

    def greet(j):
        i = (me32 + j) % 32
        pl.semaphore_signal(
            barrier, inc=1, device_id=(i // 16, y * 2 + i % 2, (i // 2) % 8), device_id_type=MESH
        )

    loop(1, 32, greet)

    def greet_y(j):
        i = (y * 2 + j) % 8
        pl.semaphore_signal(barrier, inc=1, device_id=(dp, i - i % 2 + (j % 2), t), device_id_type=MESH)

    loop(2, 8, greet_y)
    mine = dp * 2 + c
    metas[mine, 0:2, :] = ids[...].astype(F32)
    metas[mine, 2:4, :] = rw[...]
    pl.semaphore_wait(barrier, 37)

    zn = (1 - dp, 1 - zlo)
    tn = (1 - zlo) * 4 + x

    def met_copy(j):
        dev = ((dp, y * 2 + 1 - c, t), (1 - dp, y * 2 + c, tn), (1 - dp, y * 2 + 1 - c, tn))[j]
        return at(metas.at[mine], metas.at[mine], met_ss.at[j], met_rs.at[mine], dev)

    for j in range(3):
        met_copy(j).start()

    grow = pl.multiple_of(mine * GRP, GRP)
    trow = pl.multiple_of(mine * GRP + t * 16, 16)

    def tok_copy(j):
        h = dp if j == 0 else 1 - dp
        dev = (dp, y * 2, t) if j == 0 else (1 - dp, y * 2, tn)
        return at(
            tok.at[:, pl.ds(pl.multiple_of(h * half, half), half)],
            gat.at[pl.ds(grow, GRP), :],
            tok_ss.at[j],
            tok_rs.at[mine],
            dev,
        )

    me16 = dp * 8 + t
    sidx = mine * 8 + t

    def cot_copy(j):
        i = (me16 + j) % 16
        return at(
            cot.at[:, pl.ds(pl.multiple_of((i // 8) * half, half), half)],
            gat.at[pl.ds(trow, 16), :],
            cot_ss.at[j],
            cot_rs.at[sidx],
            (i // 8, y * 2 + 1, i % 8),
        )

    tok_copy(1).start()
    loop(1, 16, lambda j: cot_copy(j).start())

    @pl.when(c == 1)
    def _():
        tok_copy(0).start()
        gat[pl.ds(trow, 16), :] = cot[:, pl.ds(pl.multiple_of(dp * half, half), half)]

    @pl.when(c == 0)
    def _():
        cot_copy(0).start()
        gat[pl.ds(grow, GRP), :] = tok[:, pl.ds(pl.multiple_of(dp * half, half), half)]

    def met_wait(j):
        g = (mine + j) % 4
        at(metas.at[g], metas.at[g], met_ss.at[0], met_rs.at[g], (dp, y * 2 + 1 - c, t)).wait_recv()

    loop(1, 4, met_wait)
    eio = lax.broadcasted_iota(jnp.int32, (8, GRP), 0).astype(F32)
    tri = (
        lax.broadcasted_iota(jnp.int32, (GRP, GRP), 0) < lax.broadcasted_iota(jnp.int32, (GRP, GRP), 1)
    ).astype(F32).astype(BF)
    for g in range(4):
        mg = metas[g]
        h0 = mg[0:1, :] == eio
        h1 = mg[1:2, :] == eio
        hot = jnp.where(h0, 1.0, jnp.where(h1, 1.0, 0.0))
        slot = jnp.dot(hot.astype(BF), tri, preferred_element_type=F32)
        sc = jnp.where(hot > 0.5, slot + float(g * CAP), -1.0)
        rc = jnp.where(h0, mg[2:3, :], jnp.where(h1, mg[3:4, :], 0.0))
        for k in range(8):
            slotcol[k, 0:1, g * GRP : (g + 1) * GRP] = sc[k : k + 1, :]
            rwcol[k, 0:1, g * GRP : (g + 1) * GRP] = rc[k : k + 1, :]

    def one_hot(ex):
        rio = lax.broadcasted_iota(jnp.int32, (RC, TOKC), 0).astype(F32)
        return rio == slotcol[ex]

    @pl.when(c == 0)
    def _():
        def wait(j):
            g = (mine + j) % 4
            at(
                gat.at[pl.ds(pl.multiple_of(g * GRP, GRP), GRP), :],
                gat.at[pl.ds(pl.multiple_of(g * GRP, GRP), GRP), :],
                tok_ss.at[0],
                tok_rs.at[g],
                (1 - dp, e, tn),
            ).wait_recv()

        loop(1, 4, wait)

    @pl.when(c == 1)
    def _():
        def wait(j):
            i = (sidx + j) % 32
            r = pl.ds(pl.multiple_of(i * 16, 16), 16)
            at(gat.at[r, :], gat.at[r, :], cot_ss.at[0], cot_rs.at[i], (1 - dp, e, tn)).wait_recv()

        loop(1, 32, wait)

    def place(ex, dst):
        hot = one_hot(ex)
        scale = jnp.sum(jnp.where(hot, rwcol[ex], 0.0), axis=1, keepdims=True)
        scale = jnp.where(c == 0, 1.0, scale)
        hot = hot.astype(F32).astype(BF)
        for n in range(4):
            v = jnp.dot(hot, gat[:, n * xb_w : (n + 1) * xb_w], preferred_element_type=F32)
            dst[:, n * xb_w : (n + 1) * xb_w] = (v * scale).astype(BF)

    def d_copy(k, c2):
        return at(
            stage.at[k, c2],
            xd.at[c, k],
            d_ss.at[k, c2],
            d_rs.at[c, k],
            (dp, ((y + 4 - k) % 4) * 2 + c2, t),
        )

    place(y * 2 + 1 - c, stage.at[0, 1 - c])
    d_copy(0, 1 - c).start()
    place(e, xd.at[c, 0])
    for m in range(2):
        for f in range(NF):
            w_copy(m, f).wait()

    def d_wait(m, k):
        at(xd.at[m, k], xd.at[m, k], d_ss.at[0, 0], d_rs.at[m, k], (1 - dp, e, t)).wait_recv()

    d_wait(1 - c, 0)

    other = (1 - dp, e, t)

    def z_copy(k, f):
        return at(zs.at[k, f], zr.at[k, f], z_ss.at[k, f], z_rs.at[k, f], other)

    def x_copy(m, k):
        return pltpu.make_async_copy(
            xd.at[m, k], xd_hbm.at[m, pl.ds(pl.multiple_of(k * RC, RC), RC), :], x_sem.at[m, k]
        )

    def project(k):
        s = k % 2

        def piece(f):
            for m in range(2):
                v = jnp.dot(xd[m, k], w[m, f], preferred_element_type=F32)
                own[s, f, m] = v
                zs[k, f, m] = v.astype(BF)
            z_copy(k, f).start()

        loop(0, NF, piece)
        for m in range(2):
            x_copy(m, k).start()

    project(0)

    def dispatch(i):
        k, c2 = i // 2, i % 2
        place(((y + 4 - k) % 4) * 2 + c2, stage.at[k, c2])
        d_copy(k, c2).start()

    loop(2, 8, dispatch)

    def ad_copy(m, k, f):
        return pltpu.make_async_copy(
            ad.at[k, f, m],
            ad_hbm.at[m, pl.ds(pl.multiple_of(k * RC, RC), RC), pl.ds(pl.multiple_of(f * fc, fc), fc)],
            o_sem.at[m, k, f],
        )

    def c1_copy(k, j):
        xb = (x + j) % 4
        return at(c1s.at[k, xb], c1r.at[k, x], c1_ss.at[k, j], c1_rs.at[k, x], (dp, e, zlo * 4 + xb))

    def c2_copy(k):
        return at(c2s.at[k], res.at[y], c2_ss.at[k], c2_rs.at[y], (dp, ((y + k) % 4) * 2 + c, t))

    def chunk(k):
        @pl.when(k < 3)
        def _():
            d_wait(0, k + 1)
            d_wait(1, k + 1)
            project(k + 1)

        s = k % 2
        acc[...] = jnp.zeros_like(acc)

        def piece(f):
            z_copy(k, f).wait_recv()
            up = own[s, f, 0] + zr[k, f, 0].astype(F32)
            da = own[s, f, 1] + zr[k, f, 1].astype(F32)
            sg = jax.nn.sigmoid(up)
            ad[k, f, 0] = (up * sg).astype(BF)
            du = (da * sg * (1.0 + up * (1.0 - sg))).astype(BF)
            ad[k, f, 1] = du
            ad_copy(0, k, f).start()
            ad_copy(1, k, f).start()
            for n in range(4):
                acc[n] += lax.dot_general(
                    du,
                    w[0, f, n * xb_w : (n + 1) * xb_w, :],
                    (((1,), (1,)), ((), ())),
                    preferred_element_type=F32,
                )

        loop(0, NF, piece)

        def send(j):
            xb = (x + j) % 4
            c1s[k, xb] = acc[xb].astype(BF)
            c1_copy(k, j).start()

        loop(1, 4, send)
        total = acc[x]
        for j in range(1, 4):
            xs = (x + j) % 4
            at(c1r.at[k, xs], c1r.at[k, xs], c1_ss.at[0, 0], c1_rs.at[k, xs], other).wait_recv()
            total += c1r[k, xs].astype(F32)

        @pl.when(k == 0)
        def _():
            res[y] = total.astype(BF)

        @pl.when(k > 0)
        def _():
            c2s[k] = total.astype(BF)
            c2_copy(k).start()

    loop(0, 4, chunk)

    def res_wait(k):
        i = (y + 4 - k) % 4
        at(res.at[i], res.at[i], c2_ss.at[0], c2_rs.at[i], other).wait_recv()

    loop(1, 4, res_wait)
    for g in range(4):
        total = jnp.zeros((GRP, xb_w), F32)
        for k in range(4):
            hot = lax.broadcasted_iota(jnp.int32, (RC, GRP), 0).astype(F32) == slotcol[
                k * 2 + c, :, g * GRP : (g + 1) * GRP
            ]
            total += lax.dot_general(
                hot.astype(F32).astype(BF), res[k], (((0,), (0,)), ((), ())), preferred_element_type=F32
            )
        fin_s[g * GRP : (g + 1) * GRP, :] = total.astype(fin_s.dtype)

    spot = (dp * 4 + x) * 4 + zlo * 2 + c

    def f_copy(j):
        i = (me32 + j) % 32
        d2, t2, c2 = i // 16, (i // 2) % 8, i % 2
        row = pl.multiple_of((d2 * 2 + c2) * GRP + t2 * 16, 16)
        return at(fin_s.at[pl.ds(row, 16), :], fin_r.at[spot], f_ss.at[j], f_rs.at[spot], (d2, y * 2 + c2, t2))

    loop(1, 32, lambda j: f_copy(j).start())
    fin_r[spot] = fin_s[pl.ds(pl.multiple_of(mine * GRP + t * 16, 16), 16), :]

    def f_wait(j):
        i = (spot + j) % 32
        at(fin_r.at[i], fin_r.at[i], f_ss.at[0], f_rs.at[i], other).wait_recv()

    loop(1, 32, f_wait)
    for b in range(8):
        v = fin_r[b * 4].astype(F32)
        for p in range(1, 4):
            v += fin_r[b * 4 + p].astype(F32)
        out[:, b * xb_w : (b + 1) * xb_w] = v.astype(BF)

    for j in range(3):
        met_copy(j).wait_send()
    tok_copy(1).wait_send()
    loop(1, 16, lambda j: cot_copy(j).wait_send())

    @pl.when(c == 1)
    def _():
        tok_copy(0).wait_send()

    @pl.when(c == 0)
    def _():
        cot_copy(0).wait_send()

    d_copy(0, 1 - c).wait_send()
    loop(2, 8, lambda i: d_copy(i // 2, i % 2).wait_send())

    def drain(i):
        k, f = i // NF, i % NF
        z_copy(k, f).wait_send()
        ad_copy(0, k, f).wait()
        ad_copy(1, k, f).wait()

    loop(0, 4 * NF, drain)
    loop(0, 12, lambda i: c1_copy(i // 3, 1 + i % 3).wait_send())
    loop(1, 4, lambda k: c2_copy(k).wait_send())
    loop(1, 32, lambda j: f_copy(j).wait_send())

    def x_drain(k):
        x_copy(0, k).wait()
        x_copy(1, k).wait()

    loop(0, 4, x_drain)


def shards(tokens, cotangent, expert_ids, route_weight, w_up, w_down):
    half, ff = w_up.shape[1], w_up.shape[2]
    rows = 4 * RC
    fc = ff // NF
    xb_w = half // 4
    vmem = pl.BlockSpec(memory_space=pltpu.VMEM)
    hbm = pl.BlockSpec(memory_space=pl.ANY)
    dma = pltpu.SemaphoreType.DMA
    out, xd, ad = pl.pallas_call(
        kernel,
        out_shape=(
            jax.ShapeDtypeStruct(cotangent.shape, BF),
            jax.ShapeDtypeStruct((2, rows, half), BF),
            jax.ShapeDtypeStruct((2, rows, ff), BF),
        ),
        in_specs=[vmem] * 4 + [hbm] * 2,
        out_specs=(vmem, hbm, hbm),
        scratch_shapes=[
            pltpu.VMEM((2, NF, half, fc), BF),
            pltpu.VMEM((TOKC, half), BF),
            pltpu.VMEM((4, 4, GRP), F32),
            pltpu.VMEM((8, 1, TOKC), F32),
            pltpu.VMEM((8, 1, TOKC), F32),
            pltpu.VMEM((4, 2, RC, half), BF),
            pltpu.VMEM((2, 4, RC, half), BF),
            pltpu.VMEM((2, NF, 2, RC, fc), F32),
            pltpu.VMEM((4, NF, 2, RC, fc), BF),
            pltpu.VMEM((4, NF, 2, RC, fc), BF),
            pltpu.VMEM((4, NF, 2, RC, fc), BF),
            pltpu.VMEM((4, RC, xb_w), F32),
            pltpu.VMEM((4, 4, RC, xb_w), BF),
            pltpu.VMEM((4, 4, RC, xb_w), BF),
            pltpu.VMEM((4, RC, xb_w), BF),
            pltpu.VMEM((4, RC, xb_w), BF),
            pltpu.VMEM((TOKC, xb_w), BF),
            pltpu.VMEM((32, 16, xb_w), BF),
            dma((2, NF)),
            dma((16,)),
            dma((32,)),
            dma((2,)),
            dma((4,)),
            dma((3,)),
            dma((4,)),
            dma((4, 2)),
            dma((2, 4)),
            dma((4, NF)),
            dma((4, NF)),
            dma((4, 4)),
            dma((4, 4)),
            dma((4,)),
            dma((4,)),
            dma((32,)),
            dma((32,)),
            dma((2, 4, NF)),
            dma((2, 4)),
        ],
        compiler_params=pltpu.CompilerParams(
            collective_id=0, has_side_effects=True, vmem_limit_bytes=58 * 2**20
        ),
        cost_estimate=pl.CostEstimate(
            flops=6 * rows * half * ff, bytes_accessed=4 * half * ff, transcendentals=rows * ff
        ),
    )(tokens, cotangent, expert_ids.T, route_weight.T, w_up, w_down)

    def grad(left, right):
        return lax.dot_general(
            left, right, (((0,), (0,)), ((), ())), preferred_element_type=F32
        ).astype(BF)[None]

    return out, grad(xd[0], ad[1]), grad(xd[1], ad[0])


def solution(mesh):
    placed = (
        P(("dp", "expert"), None),
        P(("dp", "expert", "tensor"), None),
        P(("dp", "expert"), None),
        P(("dp", "expert"), None),
        P("expert", "dp", "tensor"),
        P("expert", "dp", "tensor"),
    )
    return jax.shard_map(
        shards,
        mesh=mesh,
        in_specs=placed,
        out_specs=(
            P(("dp", "expert", "tensor"), None),
            P("expert", "dp", "tensor"),
            P("expert", "dp", "tensor"),
        ),
        check_vma=False,
    )
```

time: 645 us -> 174 us (0.27); the launches traced: 634 us -> 174 us
  waiting for transfers between devices: 309 us -> 0 us
  Pallas kernels: 0 us -> 157 us
  local copies, waits for them, and re-layouts: 151 us -> 0.65 us
  blocking collectives: 71.6 us -> 0 us
  starting transfers between devices: 30.6 us -> 0 us
  matrix products: 44.5 us -> 16 us
  between operations: 14.6 us -> 0.66 us
  other arithmetic: 12.3 us -> 0 us
    psum x1 -> x0, waiting for transfers between devices: 231 us -> none  [shards(): up_sum, dact_sum = lax.psum((up_part, dact_part), 'dp')]
    pallas_call x0 -> x1, Pallas kernels: none -> 157 us  [shards(): pl.pallas_call(kernel, out_shape=(jax.ShapeDtypeStruct(cotangent.shape, B...]
    unnamed x23 -> x7, local copies, waits for them, and re-layouts: 78.6 us -> 0.65 us
    all_to_all x5 -> x0, waiting for transfers between devices: 59.5 us -> none  [the longest x1 39.1 us: shards(): back = lax.all_to_all(middle, 'dp', split_axis=0, concat_axis=3, tiled=True)]
    all_to_all x1 -> x0, blocking collectives: 46.4 us -> none  [shards(): lax.all_to_all(route_part, 'expert', split_axis=1, concat_axis=1, tiled=T...]
    all_to_all x8 -> x0, local copies, waits for them, and re-layouts: 46.3 us -> none  [the longest x2 13.2 us: shards(): lax.all_to_all(recv_x, 'dp', split_axis=3, concat_axis=0, tiled=True)]
    all_to_all x5 -> x0, starting transfers between devices: 30.1 us -> none  [the longest x1 10.7 us: shards(): lax.all_to_all(send_d, 'expert', split_axis=1, concat_axis=1, tiled=True)]
    dot_general x7 -> x2, matrix products: 44.5 us -> 16 us  [grad(): lax.dot_general(left, right, (((0,), (0,)), ((), ())), preferred_element_...]
  transfers between devices with their start and end apart: 7 -> 0, of which waited for: 4 -> 0; matrix products, arithmetic and copies ran while one was open for 17% -> 0% of each run, Pallas kernels for 0% -> 0%
where the time goes in v1:
time: 174 us
  Pallas kernels  157 us (90%)
  matrix products  16 us (9%)
    pallas_call x1, Pallas kernels, shards(): pl.pallas_call(kernel, out_shape=(jax.ShapeDtypeStruct(cotangent.shape, B...  157 us
    dot_general x2, matrix products, grad(): lax.dot_general(left, right, (((0,), (0,)), ((), ())), preferred_element_...  16 us

profile of v1, /device:TPU:9, one launch (start us, length us, event | category | flops | bytes accessed | tf_op | source)
XLA Modules:
  0.0 173.9 jit_solution(17691100513410999173)
XLA Ops:
  0.6 156.6 %shard_map.85 = (bf16[16,3072]{1,0:T(8,128)(2,1)}, bf16[2,576,1536]{2,1,0:T(8,128)(2,1)}, bf16[2,576,2048]{2,1,0:T(8,128)(2,1)}) custom-call(bf16[128,3072]{1,0:T(8,128)(2,1)} %tok.1, bf16[16,3072]{1,0:T(8,128)(2,1)} %cot.1, s32[2,128]{1,0:T(2,128)} %bitcast.18, f32[2,128]{1,0:T(2,128)} %bitcast.19, bf16[1,1536,2048]{2,1,0:T(8,128)(2,1)} %wu_hbm.1, ...), custom_call_target="tpu_custom_call" | custom-call | flops 10871635968 | bytes 12582912 | tf_op jit(solution)/shard_map/pallas_call | solution.py:424
  157.3 0.0 copy-start.1
  157.3 0.0 copy-start.2
  157.3 9.0 %fusion.1 = bf16[1,1536,2048]{2,1,0:T(8,128)(2,1)} fusion(bf16[2,576,2048]{2,1,0:T(8,128)(2,1)} %get-tuple-element.8, bf16[2,576,1536]{2,1,0:T(8,128)(2,1)} %get-tuple-element.7), kind=kOutput, calls=%fused_computation.3 | convolution fusion | flops 3627024384 | bytes 10420224 | tf_op jit(solution)/shard_map/dot_general | solution.py:481
  166.2 0.0 copy-done.1
  166.2 0.0 copy-done.2
  166.2 0.0 copy-start
  166.3 7.0 %fusion = bf16[1,1536,2048]{2,1,0:T(8,128)(2,1)} fusion(bf16[2,576,2048]{2,1,0:T(8,128)(2,1)S(1)} %copy-done.1, bf16[2,576,1536]{2,1,0:T(8,128)(2,1)S(1)} %copy-done.2), kind=kOutput, calls=%fused_computation.2 | convolution fusion | flops 3627024384 | bytes 10420224 | tf_op jit(solution)/shard_map/dot_general | solution.py:481
  173.3 0.0 copy-done
  173.3 0.6 copy.10
Async XLA Ops:
  157.3 9.0 %copy-start.1 = (bf16[2,576,2048]{2,1,0:T(8,128)(2,1)S(1)}, bf16[2,576,2048]{2,1,0:T(8,128)(2,1)}, u32[]{:S(2)}) copy-start(bf16[2,576,2048]{2,1,0:T(8,128)(2,1)} %get-tuple-element.8) | copy-start | bytes 14155780
  157.3 9.0 %copy-start.2 = (bf16[2,576,1536]{2,1,0:T(8,128)(2,1)S(1)}, bf16[2,576,1536]{2,1,0:T(8,128)(2,1)}, u32[]{:S(2)}) copy-start(bf16[2,576,1536]{2,1,0:T(8,128)(2,1)} %get-tuple-element.7) | copy-start | bytes 10616836
  166.2 7.0 %copy-start = (bf16[16,3072]{1,0:T(8,128)(2,1)S(1)}, bf16[16,3072]{1,0:T(8,128)(2,1)}, u32[]{:S(2)}) copy-start(bf16[16,3072]{1,0:T(8,128)(2,1)} %get-tuple-element.12) | copy-start | bytes 294916

commit v2 on v1

--- a/solution.py
+++ b/solution.py
@@ -9,6 +9,7 @@
 GRP = 128
 RC = 4 * CAP
 TOKC = 4 * GRP
+PR = 80
 NF = 4
 MESH = pl.DeviceIdType.MESH
 BF = jnp.bfloat16
@@ -25,6 +26,7 @@
     out,
     xd_hbm,
     ad_hbm,
+    gp_hbm,
     w,
     gat,
     metas,
@@ -43,8 +45,11 @@
     res,
     fin_s,
     fin_r,
+    unhot,
+    gs,
     w_sem,
     cot_ss,
+    fwd_ss,
     cot_rs,
     tok_ss,
     tok_rs,
@@ -62,10 +67,12 @@
     f_rs,
     o_sem,
     x_sem,
+    g_sem,
 ):
     dp, e, t = lax.axis_index("dp"), lax.axis_index("expert"), lax.axis_index("tensor")
     y, c = e // 2, e % 2
     zlo, x = t // 4, t % 4
+    z = dp * 2 + zlo
     half = w.shape[2]
     fc = w.shape[3]
     xb_w = half // 4
@@ -93,27 +100,27 @@
             w_copy(m, f).start()
 
     barrier = pltpu.get_barrier_semaphore()
-    me32 = (dp * 8 + t) * 2 + c
-
-    def greet(j):
-        i = (me32 + j) % 32
-        pl.semaphore_signal(
-            barrier, inc=1, device_id=(i // 16, y * 2 + i % 2, (i // 2) % 8), device_id_type=MESH
-        )
-
-    loop(1, 32, greet)
-
-    def greet_y(j):
-        i = (y * 2 + j) % 8
-        pl.semaphore_signal(barrier, inc=1, device_id=(dp, i - i % 2 + (j % 2), t), device_id_type=MESH)
-
-    loop(2, 8, greet_y)
-    mine = dp * 2 + c
+    me16 = dp * 8 + t
+
+    def greet(d, ex, tt):
+        pl.semaphore_signal(barrier, inc=1, device_id=(d, ex, tt), device_id_type=MESH)
+
+    def greet_plane(j):
+        i = (me16 + j) % 16
+        greet(i // 8, e, i % 8)
+
+    loop(1, 16, greet_plane)
+    for j in range(4):
+        zz = (z + j) % 4
+        greet(zz // 2, y * 2 + 1 - c, (zz % 2) * 4 + x)
+    for j in range(1, 4):
+        for c2 in range(2):
+            greet(dp, ((y + j) % 4) * 2 + c2, t)
+    mine = c * 2 + dp
     metas[mine, 0:2, :] = ids[...].astype(F32)
     metas[mine, 2:4, :] = rw[...]
-    pl.semaphore_wait(barrier, 37)
-
-    zn = (1 - dp, 1 - zlo)
+    pl.semaphore_wait(barrier, 25)
+
     tn = (1 - zlo) * 4 + x
 
     def met_copy(j):
@@ -137,31 +144,61 @@
             dev,
         )
 
-    me16 = dp * 8 + t
     sidx = mine * 8 + t
 
     def cot_copy(j):
-        i = (me16 + j) % 16
+        zz = (z + j) % 4
         return at(
-            cot.at[:, pl.ds(pl.multiple_of((i // 8) * half, half), half)],
+            cot.at[:, pl.ds(pl.multiple_of((zz // 2) * half, half), half)],
             gat.at[pl.ds(trow, 16), :],
             cot_ss.at[j],
             cot_rs.at[sidx],
-            (i // 8, y * 2 + 1, i % 8),
-        )
+            (zz // 2, y * 2 + 1, (zz % 2) * 4 + x),
+        )
+
+    def shard(q, xs):
+        zz = (z + q // 2) % 4
+        return (((c + q) % 2) * 2 + zz // 2) * 8 + (zz % 2) * 4 + xs
+
+    def rows_of(i):
+        return gat.at[pl.ds(pl.multiple_of(i * 16, 16), 16), :]
+
+    def fwd_copy(q, j):
+        i = shard(q, x)
+        return at(
+            rows_of(i), rows_of(i), fwd_ss.at[q, j - 1], cot_rs.at[i], (dp, e, zlo * 4 + (x + j) % 4)
+        )
+
+    def cot_wait(i):
+        at(rows_of(i), rows_of(i), cot_ss.at[0], cot_rs.at[i], (1 - dp, e, tn)).wait_recv()
+
+    for j in range(1, 4):
+        cot_copy(j).start()
+
+    @pl.when(c == 0)
+    def _():
+        cot_copy(0).start()
 
     tok_copy(1).start()
-    loop(1, 16, lambda j: cot_copy(j).start())
+
+    @pl.when(c == 0)
+    def _():
+        gat[pl.ds(grow, GRP), :] = tok[:, pl.ds(pl.multiple_of(dp * half, half), half)]
 
     @pl.when(c == 1)
     def _():
         tok_copy(0).start()
         gat[pl.ds(trow, 16), :] = cot[:, pl.ds(pl.multiple_of(dp * half, half), half)]
 
-    @pl.when(c == 0)
-    def _():
-        cot_copy(0).start()
-        gat[pl.ds(grow, GRP), :] = tok[:, pl.ds(pl.multiple_of(dp * half, half), half)]
+        def forward(q):
+            @pl.when(q > 0)
+            def _():
+                cot_wait(shard(q, x))
+
+            for j in range(1, 4):
+                fwd_copy(q, j).start()
+
+        loop(0, 8, forward)
 
     def met_wait(j):
         g = (mine + j) % 4
@@ -204,12 +241,7 @@
 
     @pl.when(c == 1)
     def _():
-        def wait(j):
-            i = (sidx + j) % 32
-            r = pl.ds(pl.multiple_of(i * 16, 16), 16)
-            at(gat.at[r, :], gat.at[r, :], cot_ss.at[0], cot_rs.at[i], (1 - dp, e, tn)).wait_recv()
-
-        loop(1, 32, wait)
+        loop(0, 24, lambda i: cot_wait(shard(i % 8, (x + 1 + i // 8) % 4)))
 
     def place(ex, dst):
         hot = one_hot(ex)
@@ -248,7 +280,7 @@
 
     def x_copy(m, k):
         return pltpu.make_async_copy(
-            xd.at[m, k], xd_hbm.at[m, pl.ds(pl.multiple_of(k * RC, RC), RC), :], x_sem.at[m, k]
+            xd.at[m, k], xd_hbm.at[m], x_sem.at[m]
         )
 
     def project(k):
@@ -262,8 +294,6 @@
             z_copy(k, f).start()
 
         loop(0, NF, piece)
-        for m in range(2):
-            x_copy(m, k).start()
 
     project(0)
 
@@ -273,20 +303,47 @@
         d_copy(k, c2).start()
 
     loop(2, 8, dispatch)
+    cols = pl.ds(pl.multiple_of(c * 2 * GRP, 2 * GRP), 2 * GRP)
+    rio = lax.broadcasted_iota(jnp.int32, (8, PR, 2 * GRP), 1) + c * (2 * CAP)
+    hot = jnp.where(rio.astype(F32) == slotcol[:, :, cols], 1.0, 0.0).reshape(8 * PR, 2 * GRP)
+    unhot[...] = hot.T.astype(BF)
 
     def ad_copy(m, k, f):
         return pltpu.make_async_copy(
             ad.at[k, f, m],
-            ad_hbm.at[m, pl.ds(pl.multiple_of(k * RC, RC), RC), pl.ds(pl.multiple_of(f * fc, fc), fc)],
-            o_sem.at[m, k, f],
+            ad_hbm.at[m, :, pl.ds(pl.multiple_of(f * fc, fc), fc)],
+            o_sem.at[m, f],
         )
 
     def c1_copy(k, j):
         xb = (x + j) % 4
         return at(c1s.at[k, xb], c1r.at[k, x], c1_ss.at[k, j], c1_rs.at[k, x], (dp, e, zlo * 4 + xb))
 
-    def c2_copy(k):
-        return at(c2s.at[k], res.at[y], c2_ss.at[k], c2_rs.at[y], (dp, ((y + k) % 4) * 2 + c, t))
+    def c2_copy(k, c2):
+        dev = (dp, ((y + k) % 4) * 2 + c2, t)
+        return at(c2s.at[k, c2], res.at[e], c2_ss.at[k, c2], c2_rs.at[e], dev)
+
+    def g_copy(i):
+        m, f = i // NF, i % NF
+        return pltpu.make_async_copy(
+            gs.at[i % 2],
+            gp_hbm.at[m, :, pl.ds(pl.multiple_of(f * fc, fc), fc)],
+            g_sem.at[i],
+        )
+
+    def gradient(i):
+        m, f = i // NF, i % NF
+
+        @pl.when(i >= 2)
+        def _():
+            g_copy(i - 2).wait()
+
+        right = ad[0:3, f, 1 - m].reshape(3 * RC, fc)
+        for n in range(4):
+            left = xd[m, 0:3, :, n * xb_w : (n + 1) * xb_w].reshape(3 * RC, xb_w)
+            v = lax.dot_general(left, right, (((0,), (0,)), ((), ())), preferred_element_type=F32)
+            gs[i % 2, n * xb_w : (n + 1) * xb_w, :] = v.astype(BF)
+        g_copy(i).start()
 
     def chunk(k):
         @pl.when(k < 3)
@@ -294,6 +351,11 @@
             d_wait(0, k + 1)
             d_wait(1, k + 1)
             project(k + 1)
+
+        @pl.when(k == 2)
+        def _():
+            x_copy(0, 3).start()
+            x_copy(1, 3).start()
 
         s = k % 2
         acc[...] = jnp.zeros_like(acc)
@@ -306,8 +368,12 @@
             ad[k, f, 0] = (up * sg).astype(BF)
             du = (da * sg * (1.0 + up * (1.0 - sg))).astype(BF)
             ad[k, f, 1] = du
-            ad_copy(0, k, f).start()
-            ad_copy(1, k, f).start()
+
+            @pl.when(k == 3)
+            def _():
+                ad_copy(0, 3, f).start()
+                ad_copy(1, 3, f).start()
+
             for n in range(4):
                 acc[n] += lax.dot_general(
                     du,
@@ -324,69 +390,69 @@
             c1_copy(k, j).start()
 
         loop(1, 4, send)
+
+        @pl.when(k == 2)
+        def _():
+            loop(0, 2 * NF, gradient)
+
         total = acc[x]
         for j in range(1, 4):
             xs = (x + j) % 4
             at(c1r.at[k, xs], c1r.at[k, xs], c1_ss.at[0, 0], c1_rs.at[k, xs], other).wait_recv()
             total += c1r[k, xs].astype(F32)
 
-        @pl.when(k == 0)
-        def _():
-            res[y] = total.astype(BF)
-
-        @pl.when(k > 0)
-        def _():
-            c2s[k] = total.astype(BF)
-            c2_copy(k).start()
+        for c2 in range(2):
+            part = total[c2 * 2 * CAP : (c2 + 1) * 2 * CAP, :]
+            part = jnp.concatenate([part, jnp.zeros((PR - 2 * CAP, xb_w), F32)], axis=0).astype(BF)
+            own_rows = jnp.logical_and(k == 0, c == c2)
+
+            @pl.when(own_rows)
+            def _():
+                res[e] = part
+
+            @pl.when(jnp.logical_not(own_rows))
+            def _():
+                c2s[k, c2] = part
+                c2_copy(k, c2).start()
 
     loop(0, 4, chunk)
 
-    def res_wait(k):
-        i = (y + 4 - k) % 4
-        at(res.at[i], res.at[i], c2_ss.at[0], c2_rs.at[i], other).wait_recv()
-
-    loop(1, 4, res_wait)
-    for g in range(4):
-        total = jnp.zeros((GRP, xb_w), F32)
-        for k in range(4):
-            hot = lax.broadcasted_iota(jnp.int32, (RC, GRP), 0).astype(F32) == slotcol[
-                k * 2 + c, :, g * GRP : (g + 1) * GRP
-            ]
-            total += lax.dot_general(
-                hot.astype(F32).astype(BF), res[k], (((0,), (0,)), ((), ())), preferred_element_type=F32
-            )
-        fin_s[g * GRP : (g + 1) * GRP, :] = total.astype(fin_s.dtype)
-
-    spot = (dp * 4 + x) * 4 + zlo * 2 + c
+    def res_wait(j):
+        i = (e + j) % 8
+        at(res.at[i], res.at[i], c2_ss.at[0, 0], c2_rs.at[i], other).wait_recv()
+
+    loop(1, 8, res_wait)
+    back = res[...].reshape(8 * PR, xb_w)
+    fin_s[...] = jnp.dot(unhot[...], back, preferred_element_type=F32).astype(BF)
+
+    spot = (dp * 4 + x) * 2 + zlo
 
     def f_copy(j):
-        i = (me32 + j) % 32
-        d2, t2, c2 = i // 16, (i // 2) % 8, i % 2
-        row = pl.multiple_of((d2 * 2 + c2) * GRP + t2 * 16, 16)
-        return at(fin_s.at[pl.ds(row, 16), :], fin_r.at[spot], f_ss.at[j], f_rs.at[spot], (d2, y * 2 + c2, t2))
-
-    loop(1, 32, lambda j: f_copy(j).start())
-    fin_r[spot] = fin_s[pl.ds(pl.multiple_of(mine * GRP + t * 16, 16), 16), :]
+        i = (me16 + j) % 16
+        row = pl.multiple_of(i * 16, 16)
+        return at(fin_s.at[pl.ds(row, 16), :], fin_r.at[spot], f_ss.at[j], f_rs.at[spot], (i // 8, e, i % 8))
+
+    loop(1, 16, lambda j: f_copy(j).start())
+    fin_r[spot] = fin_s[pl.ds(pl.multiple_of(me16 * 16, 16), 16), :]
 
     def f_wait(j):
-        i = (spot + j) % 32
+        i = (spot + j) % 16
         at(fin_r.at[i], fin_r.at[i], f_ss.at[0], f_rs.at[i], other).wait_recv()
 
-    loop(1, 32, f_wait)
+    loop(1, 16, f_wait)
     for b in range(8):
-        v = fin_r[b * 4].astype(F32)
-        for p in range(1, 4):
-            v += fin_r[b * 4 + p].astype(F32)
+        v = fin_r[b * 2].astype(F32) + fin_r[b * 2 + 1].astype(F32)
         out[:, b * xb_w : (b + 1) * xb_w] = v.astype(BF)
 
     for j in range(3):
         met_copy(j).wait_send()
     tok_copy(1).wait_send()
-    loop(1, 16, lambda j: cot_copy(j).wait_send())
+    loop(1, 4, lambda j: cot_copy(j).wait_send())
 
     @pl.when(c == 1)
     def _():
         tok_copy(0).wait_send()
+        loop(0, 24, lambda i: fwd_copy(i // 3, 1 + i % 3).wait_send())
 
     @pl.when(c == 0)
     def _():
@@ -395,22 +461,17 @@
     d_copy(0, 1 - c).wait_send()
     loop(2, 8, lambda i: d_copy(i // 2, i % 2).wait_send())
 
-    def drain(i):
-        k, f = i // NF, i % NF
-        z_copy(k, f).wait_send()
-        ad_copy(0, k, f).wait()
-        ad_copy(1, k, f).wait()
-
-    loop(0, 4 * NF, drain)
+    loop(0, 4 * NF, lambda i: z_copy(i // NF, i % NF).wait_send())
     loop(0, 12, lambda i: c1_copy(i // 3, 1 + i % 3).wait_send())
-    loop(1, 4, lambda k: c2_copy(k).wait_send())
-    loop(1, 32, lambda j: f_copy(j).wait_send())
-
-    def x_drain(k):
-        x_copy(0, k).wait()
-        x_copy(1, k).wait()
-
-    loop(0, 4, x_drain)
+    c2_copy(0, 1 - c).wait_send()
+    loop(2, 8, lambda i: c2_copy(i // 2, i % 2).wait_send())
+    loop(1, 16, lambda j: f_copy(j).wait_send())
+    for m in range(2):
+        for f in range(NF):
+            ad_copy(m, 3, f).wait()
+        x_copy(m, 3).wait()
+    g_copy(2 * NF - 2).wait()
+    g_copy(2 * NF - 1).wait()
 
 
 def shards(tokens, cotangent, expert_ids, route_weight, w_up, w_down):
@@ -421,15 +482,16 @@
     vmem = pl.BlockSpec(memory_space=pltpu.VMEM)
     hbm = pl.BlockSpec(memory_space=pl.ANY)
     dma = pltpu.SemaphoreType.DMA
-    out, xd, ad = pl.pallas_call(
+    out, xd, ad, gp = pl.pallas_call(
         kernel,
         out_shape=(
             jax.ShapeDtypeStruct(cotangent.shape, BF),
-            jax.ShapeDtypeStruct((2, rows, half), BF),
-            jax.ShapeDtypeStruct((2, rows, ff), BF),
+            jax.ShapeDtypeStruct((2, RC, half), BF),
+            jax.ShapeDtypeStruct((2, RC, ff), BF),
+            jax.ShapeDtypeStruct((2, half, ff), BF),
         ),
         in_specs=[vmem] * 4 + [hbm] * 2,
-        out_specs=(vmem, hbm, hbm),
+        out_specs=(vmem, hbm, hbm, hbm),
         scratch_shapes=[
             pltpu.VMEM((2, NF, half, fc), BF),
             pltpu.VMEM((TOKC, half), BF),
@@ -445,12 +507,15 @@
             pltpu.VMEM((4, RC, xb_w), F32),
             pltpu.VMEM((4, 4, RC, xb_w), BF),
             pltpu.VMEM((4, 4, RC, xb_w), BF),
-            pltpu.VMEM((4, RC, xb_w), BF),
-            pltpu.VMEM((4, RC, xb_w), BF),
-            pltpu.VMEM((TOKC, xb_w), BF),
-            pltpu.VMEM((32, 16, xb_w), BF),
+            pltpu.VMEM((4, 2, PR, xb_w), BF),
+            pltpu.VMEM((8, PR, xb_w), BF),
+            pltpu.VMEM((2 * GRP, xb_w), BF),
+            pltpu.VMEM((16, 16, xb_w), BF),
+            pltpu.VMEM((2 * GRP, 8 * PR), BF),
+            pltpu.VMEM((2, half, fc), BF),
             dma((2, NF)),
-            dma((16,)),
+            dma((4,)),
+            dma((8, 3)),
             dma((32,)),
             dma((2,)),
             dma((4,)),
@@ -462,12 +527,13 @@
             dma((4, NF)),
             dma((4, 4)),
             dma((4, 4)),
-            dma((4,)),
-            dma((4,)),
-            dma((32,)),
-            dma((32,)),
-            dma((2, 4, NF)),
-            dma((2, 4)),
+            dma((4, 2)),
+            dma((8,)),
+            dma((16,)),
+            dma((16,)),
+            dma((2, NF)),
+            dma((2,)),
+            dma((2 * NF,)),
         ],
         compiler_params=pltpu.CompilerParams(
             collective_id=0, has_side_effects=True, vmem_limit_bytes=58 * 2**20
@@ -477,12 +543,11 @@
         ),
     )(tokens, cotangent, expert_ids.T, route_weight.T, w_up, w_down)
 
-    def grad(left, right):
-        return lax.dot_general(
-            left, right, (((0,), (0,)), ((), ())), preferred_element_type=F32
-        ).astype(BF)[None]
-
-    return out, grad(xd[0], ad[1]), grad(xd[1], ad[0])
+    def grad(part, left, right):
+        last = lax.dot_general(left, right, (((0,), (0,)), ((), ())), preferred_element_type=F32)
+        return (part.astype(F32) + last).astype(BF)[None]
+
+    return out, grad(gp[0], xd[0], ad[1]), grad(gp[1], xd[1], ad[0])
 
 
 def solution(mesh):

time: 174 us -> 164 us (0.943)
  Pallas kernels: 157 us -> 148 us
  matrix products: 16 us -> 13 us
    pallas_call x1, Pallas kernels: 157 us -> 148 us  [shards(): pl.pallas_call(kernel, out_shape=(jax.ShapeDtypeStruct(cotangent.shape, B...]
    dot_general x2, matrix products: 16 us -> 13 us  [grad(): lax.dot_general(left, right, (((0,), (0,)), ((), ())), preferred_element_...]
where the time goes in v2:
time: 164 us; the launch traced here: 163 us
  Pallas kernels  148 us (90%)
  matrix products  13 us (8%)
    pallas_call x1, Pallas kernels, shards(): pl.pallas_call(kernel, out_shape=(jax.ShapeDtypeStruct(cotangent.shape, B...  148 us
    dot_general x2, matrix products, grad(): lax.dot_general(left, right, (((0,), (0,)), ((), ())), preferred_element_...  13 us

profile of v2, /device:TPU:9, one launch (start us, length us, event | category | flops | bytes accessed | tf_op | source)
XLA Modules:
  0.0 162.8 jit_solution(871649873598110326)
XLA Ops:
  0.6 147.8 %shard_map.85 = (bf16[16,3072]{1,0:T(8,128)(2,1)}, bf16[2,144,1536]{2,1,0:T(8,128)(2,1)}, bf16[2,144,2048]{2,1,0:T(8,128)(2,1)}, bf16[2,1536,2048]{2,1,0:T(8,128)(2,1)}) custom-call(bf16[128,3072]{1,0:T(8,128)(2,1)} %tok.1, bf16[16,3072]{1,0:T(8,128)(2,1)} %cot.1, s32[2,128]{1,0:T(2,128)} %bitcast.24, f32[2,128]{1,0:T(2,128)} %bitcast.25, ...), custom_call_target="tpu_custom_call" | custom-call | flops 10871635968 | bytes 12582912 | tf_op jit(solution)/shard_map/pallas_call | solution.py:485
  148.4 0.0 copy-start
  148.4 0.0 copy-start.1
  148.5 8.2 %fusion.3 = bf16[1,1536,2048]{2,1,0:T(8,128)(2,1)} fusion(bf16[2,1536,2048]{2,1,0:T(8,128)(2,1)} %get-tuple-element.8, bf16[2,144,2048]{2,1,0:T(8,128)(2,1)} %get-tuple-element.10, bf16[2,144,1536]{2,1,0:T(8,128)(2,1)} %get-tuple-element.9), kind=kOutput, calls=%fused_computation.5 | convolution fusion | flops 915406848 | bytes 13615104 | tf_op jit(solution)/shard_map/dot_general | solution.py:547
  156.6 0.0 copy-done
  156.6 0.7 copy-done.1
  157.3 0.0 copy-start.2
  157.3 4.9 %fusion.2 = bf16[1,1536,2048]{2,1,0:T(8,128)(2,1)} fusion(bf16[2,1536,2048]{2,1,0:T(8,128)(2,1)S(1)} %copy-done, bf16[2,144,2048]{2,1,0:T(8,128)(2,1)} %get-tuple-element.10, bf16[2,144,1536]{2,1,0:T(8,128)(2,1)S(1)} %copy-done.1), kind=kOutput, calls=%fused_computation.4 | convolution fusion | flops 915406848 | bytes 13615104 | tf_op jit(solution)/shard_map/dot_general | solution.py:547
  162.1 0.0 copy-done.2
  162.1 0.6 copy.10
Async XLA Ops:
  148.4 8.2 %copy-start = (bf16[2,1536,2048]{2,1,0:T(8,128)(2,1)S(1)}, bf16[2,1536,2048]{2,1,0:T(8,128)(2,1)}, u32[]{:S(2)}) copy-start(bf16[2,1536,2048]{2,1,0:T(8,128)(2,1)} %get-tuple-element.8) | copy-start | bytes 37748740
  148.4 8.8 %copy-start.1 = (bf16[2,144,1536]{2,1,0:T(8,128)(2,1)S(1)}, bf16[2,144,1536]{2,1,0:T(8,128)(2,1)}, u32[]{:S(2)}) copy-start(bf16[2,144,1536]{2,1,0:T(8,128)(2,1)} %get-tuple-element.9) | copy-start | bytes 2654212
  157.3 4.9 %copy-start.2 = (bf16[16,3072]{1,0:T(8,128)(2,1)S(1)}, bf16[16,3072]{1,0:T(8,128)(2,1)}, u32[]{:S(2)}) copy-start(bf16[16,3072]{1,0:T(8,128)(2,1)} %get-tuple-element.14) | copy-start | bytes 294916

commit v3 on v2

v3 whole, which is shorter than its diff:
```python
import jax
import jax.numpy as jnp
from jax import lax
from jax.experimental import pallas as pl
from jax.experimental.pallas import tpu as pltpu
from jax.sharding import PartitionSpec as P

CAP = 36
GRP = 128
RC = 4 * CAP
TOKC = 4 * GRP
PR = 80
NG = 4
NF = 4
WHOLE = (0, RC)
PLACED = ((0, 64), (64, 80))
EARLY = (0, 128)
LATE = (128, 16)
FIN = RC + LATE[1]
UNITS = ((0, (0, 64)), (0, (64, 64)), (1, WHOLE), (2, WHOLE), (3, WHOLE), (0, LATE))
SUMS = ((0, EARLY), (1, WHOLE), (2, WHOLE), (3, WHOLE), (0, (RC, LATE[1])))
AWAY = (0, 1, 3, 2)
MESH = pl.DeviceIdType.MESH
BF = jnp.bfloat16
F32 = jnp.float32


def kernel(
    tok,
    cot,
    ids,
    rw,
    wu_hbm,
    wd_hbm,
    out,
    xd_hbm,
    ad_hbm,
    gu_hbm,
    gd_hbm,
    w,
    gat,
    metas,
    slotcol,
    rwcol,
    xd,
    own,
    zs,
    zr,
    ad,
    acc,
    c1s,
    c1r,
    c2s,
    res,
    fin_s,
    fin_r,
    unhot,
    held,
    turned,
    gs,
    w_sem,
    cot_ss,
    fwd_ss,
    cot_rs,
    tok_ss,
    tok_rs,
    met_ss,
    met_rs,
    d0_ss,
    d0_rs,
    d_ss,
    d_rs,
    z_ss,
    z_rs,
    c1_ss,
    c1_rs,
    c2_ss,
    c2_rs,
    f_ss,
    f_rs,
    o_sem,
    x_sem,
    g_sem,
):
    dp, e, t = lax.axis_index("dp"), lax.axis_index("expert"), lax.axis_index("tensor")
    y, c = e // 2, e % 2
    zlo, x = t // 4, t % 4
    z = dp * 2 + zlo
    half = w.shape[2]
    fc = w.shape[3]
    xb_w = half // 4
    gc = NF * fc // NG

    def at(src, dst, ss, rs, dev):
        return pltpu.make_async_remote_copy(
            src_ref=src, dst_ref=dst, send_sem=ss, recv_sem=rs, device_id=dev, device_id_type=MESH
        )

    def loop(lo, hi, fn):
        def step(i, carry):
            fn(i)
            return carry

        lax.fori_loop(lo, hi, step, 0)

    def w_copy(m, f):
        src = wu_hbm if m == 0 else wd_hbm
        return pltpu.make_async_copy(
            src.at[0, :, pl.ds(pl.multiple_of(f * fc, fc), fc)], w.at[m, f], w_sem.at[m, f]
        )

    for m in range(2):
        for f in range(NF):
            w_copy(m, f).start()

    barrier = pltpu.get_barrier_semaphore()
    me16 = dp * 8 + t

    def greet(d, ex, tt):
        pl.semaphore_signal(barrier, inc=1, device_id=(d, ex, tt), device_id_type=MESH)

    def greet_plane(j):
        i = (me16 + j) % 16
        greet(i // 8, e, i % 8)

    loop(1, 16, greet_plane)
    for j in range(4):
        zz = (z + j) % 4
        greet(zz // 2, y * 2 + 1 - c, (zz % 2) * 4 + x)
    for j in range(1, 4):
        for c2 in range(2):
            greet(dp, ((y + j) % 4) * 2 + c2, t)
    mine = c * 2 + dp
    metas[mine, 0:2, :] = ids[...].astype(F32)
    metas[mine, 2:4, :] = rw[...]
    pl.semaphore_wait(barrier, 25)

    tn = (1 - zlo) * 4 + x

    def met_copy(j):
        dev = ((dp, y * 2 + 1 - c, t), (1 - dp, y * 2 + c, tn), (1 - dp, y * 2 + 1 - c, tn))[j]
        return at(metas.at[mine], metas.at[mine], met_ss.at[j], met_rs.at[mine], dev)

    for j in range(3):
        met_copy(j).start()

    grow = pl.multiple_of(mine * GRP, GRP)
    trow = pl.multiple_of(mine * GRP + t * 16, 16)

    def tok_copy(j):
        h = dp if j == 0 else 1 - dp
        dev = (dp, y * 2, t) if j == 0 else (1 - dp, y * 2, tn)
        return at(
            tok.at[:, pl.ds(pl.multiple_of(h * half, half), half)],
            gat.at[pl.ds(grow, GRP), :],
            tok_ss.at[j],
            tok_rs.at[mine],
            dev,
        )

    sidx = mine * 8 + t

    def cot_copy(j):
        zz = (z + j) % 4
        return at(
            cot.at[:, pl.ds(pl.multiple_of((zz // 2) * half, half), half)],
            gat.at[pl.ds(trow, 16), :],
            cot_ss.at[j],
            cot_rs.at[sidx],
            (zz // 2, y * 2 + 1, (zz % 2) * 4 + x),
        )

    def shard(q, xs):
        zz = (z + q) % 4
        return ((q // 4) * 2 + zz // 2) * 8 + (zz % 2) * 4 + xs

    def rows_of(i):
        return gat.at[pl.ds(pl.multiple_of(i * 16, 16), 16), :]

    def fwd_copy(q, j):
        i = shard(q, x)
        return at(
            rows_of(i), rows_of(i), fwd_ss.at[q, j - 1], cot_rs.at[i], (dp, e, zlo * 4 + (x + j) % 4)
        )

    def cot_wait(i):
        at(rows_of(i), rows_of(i), cot_ss.at[0], cot_rs.at[i], (1 - dp, e, tn)).wait_recv()

    for j in range(1, 4):
        cot_copy(j).start()

    @pl.when(c == 0)
    def _():
        cot_copy(0).start()
        tok_copy(1).start()
        gat[pl.ds(grow, GRP), :] = tok[:, pl.ds(pl.multiple_of(dp * half, half), half)]

    @pl.when(c == 1)
    def _():
        gat[pl.ds(trow, 16), :] = cot[:, pl.ds(pl.multiple_of(dp * half, half), half)]

        def forward(q):
            @pl.when(q != 4)
            def _():
                cot_wait(shard(q, x))

            for j in range(1, 4):
                fwd_copy(q, j).start()

        loop(0, 8, forward)
        tok_copy(1).start()
        tok_copy(0).start()

    def met_wait(j):
        g = (mine + j) % 4
        at(metas.at[g], metas.at[g], met_ss.at[0], met_rs.at[g], (dp, y * 2 + 1 - c, t)).wait_recv()

    loop(1, 4, met_wait)
    eio = lax.broadcasted_iota(jnp.int32, (8, GRP), 0).astype(F32)
    tri = (
        lax.broadcasted_iota(jnp.int32, (GRP, GRP), 0) < lax.broadcasted_iota(jnp.int32, (GRP, GRP), 1)
    ).astype(F32).astype(BF)
    for g in range(4):
        mg = metas[g]
        h0 = mg[0:1, :] == eio
        h1 = mg[1:2, :] == eio
        hot = jnp.where(h0, 1.0, jnp.where(h1, 1.0, 0.0))
        slot = jnp.dot(hot.astype(BF), tri, preferred_element_type=F32)
        sc = jnp.where(hot > 0.5, slot + float(g * CAP), -1.0)
        rc = jnp.where(h0, mg[2:3, :], jnp.where(h1, mg[3:4, :], 0.0))
        for k in range(8):
            slotcol[k, 0:1, g * GRP : (g + 1) * GRP] = sc[k : k + 1, :]
            rwcol[k, 0:1, g * GRP : (g + 1) * GRP] = rc[k : k + 1, :]

    def tok_wait(g):
        group = gat.at[pl.ds(pl.multiple_of(g * GRP, GRP), GRP), :]
        at(group, group, tok_ss.at[0], tok_rs.at[g], (1 - dp, e, tn)).wait_recv()

    def gathered(c2):
        @pl.when(c == 0)
        def _():
            if c2 == 0:
                tok_wait(1 - dp)
            else:
                tok_wait(2)
                tok_wait(3)

        @pl.when(c == 1)
        def _():
            loop(0, 12, lambda i: cot_wait(shard(c2 * 4 + i % 4, (x + 1 + i // 4) % 4)))

    def stage(k, c2):
        return ad.at[k, c2, :, pl.ds(0, half)]

    def place(ex, dst, r0, nr, nc):
        rio = lax.broadcasted_iota(jnp.int32, (nr, nc), 0) + r0
        hot = rio.astype(F32) == slotcol[ex, :, 0:nc]
        scale = jnp.sum(jnp.where(hot, rwcol[ex, :, 0:nc], 0.0), axis=1, keepdims=True)
        scale = jnp.where(c == 0, 1.0, scale)
        hot = hot.astype(F32).astype(BF)
        for n in range(4):
            v = jnp.dot(hot, gat[0:nc, n * xb_w : (n + 1) * xb_w], preferred_element_type=F32)
            dst[r0 : r0 + nr, n * xb_w : (n + 1) * xb_w] = (v * scale).astype(BF)

    def away(k):
        return jnp.where(k == 2, 3, jnp.where(k == 3, 2, k))

    def d_copy(k, c2):
        return at(
            stage(k, c2),
            xd.at[c, k],
            d_ss.at[k, c2],
            d_rs.at[c, k],
            (dp, ((y + 4 - away(k)) % 4) * 2 + c2, t),
        )

    def d_wait(m, k):
        at(xd.at[m, k], xd.at[m, k], d_ss.at[0, 0], d_rs.at[m, k], (1 - dp, e, t)).wait_recv()

    def d0_copy(p, m):
        r = pl.ds(*PLACED[p])
        return at(
            ad.at[0, 1 - c, r, pl.ds(0, half)], xd.at[m, 0, r], d0_ss.at[p], d0_rs.at[p], (dp, y * 2 + 1 - c, t)
        )

    def first(p):
        gathered(p)
        r0, nr = PLACED[p]
        nc = (p + 1) * 2 * GRP
        place(y * 2 + 1 - c, stage(0, 1 - c), r0, nr, nc)
        d0_copy(p, c).start()
        place(e, xd.at[c, 0], r0, nr, nc)

    other = (1 - dp, e, t)

    def z_copy(u, k, r0, nr, f):
        r = pl.ds(r0, nr)
        return at(zs.at[k % 2, f, :, r], zr.at[k, f, :, r], z_ss.at[u, f], z_rs.at[u, f], other)

    def x_copy(m, p):
        if p == 0:
            return pltpu.make_async_copy(xd.at[m, 3], xd_hbm.at[m, pl.ds(0, RC)], x_sem.at[m, p])
        return pltpu.make_async_copy(
            xd.at[m, 0, pl.ds(*LATE)], xd_hbm.at[m, pl.ds(RC, LATE[1])], x_sem.at[m, p]
        )

    def z_left(u):
        k, part = UNITS[u]
        loop(0, NF, lambda f: z_copy(u, k, *part, f).wait_send())

    def project(u):
        k, (r0, nr) = UNITS[u]
        s = k % 2

        def piece(f):
            for m in range(2):
                v = jnp.dot(xd[m, k, r0 : r0 + nr], w[m, f], preferred_element_type=F32)
                own[s, f, m, r0 : r0 + nr] = v
                zs[s, f, m, r0 : r0 + nr] = v.astype(BF)
            z_copy(u, k, r0, nr, f).start()

        loop(0, NF, piece)

    first(0)
    for m in range(2):
        for f in range(NF):
            w_copy(m, f).wait()
    d0_copy(0, 1 - c).wait_recv()
    project(0)
    first(1)
    d0_copy(1, 1 - c).wait_recv()
    project(1)

    def dispatch(i):
        k, c2 = i // 2, i % 2
        place(((y + 4 - away(k)) % 4) * 2 + c2, stage(k, c2), 0, RC, TOKC)
        d_copy(k, c2).start()

    loop(2, 8, dispatch)
    cols = pl.ds(pl.multiple_of(c * 2 * GRP, 2 * GRP), 2 * GRP)
    rio = lax.broadcasted_iota(jnp.int32, (8, PR, 2 * GRP), 1) + c * (2 * CAP)
    hot = jnp.where(rio.astype(F32) == slotcol[:, :, cols], 1.0, 0.0).reshape(8 * PR, 2 * GRP)
    unhot[...] = hot.T.astype(BF)

    def ad_copy(m, p, f):
        cols = pl.ds(pl.multiple_of(f * fc, fc), fc)
        if p == 0:
            src, dst = ad.at[3, m, :, cols], ad_hbm.at[m, pl.ds(0, RC), cols]
        else:
            src, dst = ad.at[0, m, pl.ds(*LATE), cols], ad_hbm.at[m, pl.ds(RC, LATE[1]), cols]
        return pltpu.make_async_copy(src, dst, o_sem.at[m, p, f])

    def c1_copy(v, k, r0, nr, j):
        xb = (x + j) % 4
        r = pl.ds(r0, nr)
        return at(
            c1s.at[xb, r], c1r.at[v % 2, x, r], c1_ss.at[v, j], c1_rs.at[v, x], (dp, e, zlo * 4 + xb)
        )

    def c2_copy(k, c2):
        dev = (dp, ((y + AWAY[k]) % 4) * 2 + c2, t)
        return at(c2s.at[k, c2], res.at[e], c2_ss.at[k, c2], c2_rs.at[e], dev)

    def g_copy(m, i):
        dst = gu_hbm if m == 0 else gd_hbm
        rows = pl.ds(pl.multiple_of((i // NG) * xb_w, xb_w), xb_w)
        cols = pl.ds(pl.multiple_of((i % NG) * gc, gc), gc)
        return pltpu.make_async_copy(gs.at[i % 2], dst.at[rows, cols], g_sem.at[m, i % 2])

    def gradients(m, lo, hi):
        def band(n):
            rows = pl.ds(pl.multiple_of(n * xb_w, xb_w), xb_w)
            turned[...] = xd[m, 0:3, :, rows].reshape(3 * RC, xb_w).T
            turned[:, LATE[0] : RC] = jnp.zeros((xb_w, LATE[1]), BF)

            def tile(f):
                i = n * NG + f

                @pl.when(i >= 2)
                def _():
                    g_copy(m, i - 2).wait()

                if m == 1:

                    @pl.when(i < 2)
                    def _():
                        g_copy(0, i + 4 * NG - 2).wait()

                cols = pl.ds(pl.multiple_of(f * gc, gc), gc)
                right = ad[0:3, 1 - m, :, cols].reshape(3 * RC, gc)
                v = jnp.dot(turned[...], right, preferred_element_type=F32)
                gs[i % 2] = v.astype(BF)
                g_copy(m, i).start()

            loop(0, NG, tile)

        loop(lo, hi, band)

    def absorb(u):
        k, (r0, nr) = UNITS[u]
        s = k % 2
        r = slice(r0, r0 + nr)
        ar = slice(RC, RC + nr) if u == 5 else r
        acc[:, ar] = jnp.zeros((4, nr, xb_w), F32)

        def piece(f):
            z_copy(u, k, r0, nr, f).wait_recv()
            up = own[s, f, 0, r] + zr[k, f, 0, r].astype(F32)
            da = own[s, f, 1, r] + zr[k, f, 1, r].astype(F32)
            sg = jax.nn.sigmoid(up)
            cols = pl.ds(pl.multiple_of(f * fc, fc), fc)
            ad[k, 0, r, cols] = (up * sg).astype(BF)
            du = (da * sg * (1.0 + up * (1.0 - sg))).astype(BF)
            ad[k, 1, r, cols] = du
            if u >= 4:
                ad_copy(0, u - 4, f).start()
                ad_copy(1, u - 4, f).start()
            for n in range(4):
                acc[n, ar] += lax.dot_general(
                    du,
                    w[0, f, n * xb_w : (n + 1) * xb_w, :],
                    (((1,), (1,)), ((), ())),
                    preferred_element_type=F32,
                )

        loop(0, NF, piece)

    def c1_left(v):
        k, part = SUMS[v]
        loop(1, 4, lambda j: c1_copy(v, k, *part, j).wait_send())

    def spread(v):
        k, (r0, nr) = SUMS[v]
        if 0 < v < 4:
            c1_left(v - 1)

        def send(j):
            xb = (x + j) % 4
            c1s[xb, r0 : r0 + nr] = acc[xb, r0 : r0 + nr].astype(BF)
            c1_copy(v, k, r0, nr, j).start()

        loop(1, 4, send)

    def collect(v):
        k, (r0, nr) = SUMS[v]
        total = acc[x, r0 : r0 + nr]
        for j in range(1, 4):
            xs = (x + j) % 4
            r = c1r.at[v % 2, xs, pl.ds(r0, nr)]
            at(r, r, c1_ss.at[0, 0], c1_rs.at[v, xs], other).wait_recv()
            total += c1r[v % 2, xs, r0 : r0 + nr].astype(F32)
        return total

    def give_back(k, c2, part):
        part = jnp.concatenate([part, jnp.zeros((PR - 2 * CAP, xb_w), F32)], axis=0).astype(BF)
        if k > 0:
            c2s[k, c2] = part
            c2_copy(k, c2).start()
        else:

            @pl.when(c == c2)
            def _():
                res[e] = part

            @pl.when(c != c2)
            def _():
                c2s[k, c2] = part
                c2_copy(k, c2).start()

    for k in range(4):
        if k < 3:
            d_wait(0, k + 1)
            d_wait(1, k + 1)
            if k == 1:
                z_left(0)
                z_left(1)
            if k == 2:
                z_left(2)
            project(k + 2)
        else:
            for m in range(2):
                for p in range(2):
                    x_copy(m, p).start()
            z_left(3)
            project(5)
        if k == 0:
            d0_copy(0, c).wait_send()
            d0_copy(1, c).wait_send()
            absorb(0)
            absorb(1)
        else:
            d_copy(k, 0).wait_send()
            d_copy(k, 1).wait_send()
            absorb(k + 1)
        spread(k)
        if k == 2:
            ad[0, :, LATE[0] :] = jnp.zeros((2, LATE[1], NF * fc), BF)
            gradients(0, 0, 4)
            gradients(1, 0, 2)
        if k == 3:
            absorb(5)
            spread(4)
            gradients(1, 2, 3)
        total = collect(k)
        give_back(k, 0, total[0 : 2 * CAP])
        if k == 0:
            held[...] = total[2 * CAP :]
        else:
            give_back(k, 1, total[2 * CAP :])

    give_back(0, 1, jnp.concatenate([held[...], collect(4)], axis=0))

    def res_wait(j):
        i = (e + j) % 8
        at(res.at[i], res.at[i], c2_ss.at[0, 0], c2_rs.at[i], other).wait_recv()

    loop(1, 8, res_wait)
    back = res[...].reshape(8 * PR, xb_w)
    fin_s[...] = jnp.dot(unhot[...], back, preferred_element_type=F32).astype(BF)

    spot = (dp * 4 + x) * 2 + zlo

    def f_copy(j):
        i = (me16 + j) % 16
        row = pl.multiple_of(i * 16, 16)
        return at(fin_s.at[pl.ds(row, 16), :], fin_r.at[spot], f_ss.at[j], f_rs.at[spot], (i // 8, e, i % 8))

    loop(1, 16, lambda j: f_copy(j).start())
    fin_r[spot] = fin_s[pl.ds(pl.multiple_of(me16 * 16, 16), 16), :]

    gradients(1, 3, 4)

    def f_wait(j):
        i = (spot + j) % 16
        at(fin_r.at[i], fin_r.at[i], f_ss.at[0], f_rs.at[i], other).wait_recv()

    loop(1, 16, f_wait)
    for b in range(8):
        v = fin_r[b * 2].astype(F32) + fin_r[b * 2 + 1].astype(F32)
        out[:, b * xb_w : (b + 1) * xb_w] = v.astype(BF)

    for j in range(3):
        met_copy(j).wait_send()
    tok_copy(1).wait_send()
    loop(1, 4, lambda j: cot_copy(j).wait_send())

    @pl.when(c == 1)
    def _():
        tok_copy(0).wait_send()
        loop(0, 24, lambda i: fwd_copy(i // 3, 1 + i % 3).wait_send())

    @pl.when(c == 0)
    def _():
        cot_copy(0).wait_send()


    z_left(4)
    z_left(5)
    c1_left(3)
    c1_left(4)
    c2_copy(0, 1 - c).wait_send()
    for k in range(1, 4):
        for c2 in range(2):
            c2_copy(k, c2).wait_send()
    loop(1, 16, lambda j: f_copy(j).wait_send())
    for m in range(2):
        for f in range(NF):
            ad_copy(m, 0, f).wait()
            ad_copy(m, 1, f).wait()
        x_copy(m, 0).wait()
        x_copy(m, 1).wait()
    g_copy(1, 4 * NG - 2).wait()
    g_copy(1, 4 * NG - 1).wait()


def finish(up_part, down_part, xd, ad, gu, gd):
    for m, (part, dst) in enumerate(((up_part, gu), (down_part, gd))):
        last = lax.dot_general(
            xd[m], ad[1 - m], (((0,), (0,)), ((), ())), preferred_element_type=F32
        )
        dst[...] = (part[...].astype(F32) + last).astype(BF)


def shards(tokens, cotangent, expert_ids, route_weight, w_up, w_down):
    half, ff = w_up.shape[1], w_up.shape[2]
    rows = 4 * RC
    fc = ff // NF
    xb_w = half // 4
    vmem = pl.BlockSpec(memory_space=pltpu.VMEM)
    hbm = pl.BlockSpec(memory_space=pl.ANY)
    dma = pltpu.SemaphoreType.DMA
    grad = jax.ShapeDtypeStruct((half, ff), BF)
    out, xd, ad, gu, gd = pl.pallas_call(
        kernel,
        out_shape=(
            jax.ShapeDtypeStruct(cotangent.shape, BF),
            jax.ShapeDtypeStruct((2, FIN, half), BF),
            jax.ShapeDtypeStruct((2, FIN, ff), BF),
            grad,
            grad,
        ),
        in_specs=[vmem] * 4 + [hbm] * 2,
        out_specs=(vmem, hbm, hbm, hbm, hbm),
        scratch_shapes=[
            pltpu.VMEM((2, NF, half, fc), BF),
            pltpu.VMEM((TOKC, half), BF),
            pltpu.VMEM((4, 4, GRP), F32),
            pltpu.VMEM((8, 1, TOKC), F32),
            pltpu.VMEM((8, 1, TOKC), F32),
            pltpu.VMEM((2, 4, RC, half), BF),
            pltpu.VMEM((2, NF, 2, RC, fc), F32),
            pltpu.VMEM((2, NF, 2, RC, fc), BF),
            pltpu.VMEM((4, NF, 2, RC, fc), BF),
            pltpu.VMEM((4, 2, RC, ff), BF),
            pltpu.VMEM((4, FIN, xb_w), F32),
            pltpu.VMEM((4, FIN, xb_w), BF),
            pltpu.VMEM((2, 4, FIN, xb_w), BF),
            pltpu.VMEM((4, 2, PR, xb_w), BF),
            pltpu.VMEM((8, PR, xb_w), BF),
            pltpu.VMEM((2 * GRP, xb_w), BF),
            pltpu.VMEM((16, 16, xb_w), BF),
            pltpu.VMEM((2 * GRP, 8 * PR), BF),
            pltpu.VMEM((EARLY[1] - 2 * CAP, xb_w), F32),
            pltpu.VMEM((xb_w, 3 * RC), BF),
            pltpu.VMEM((2, xb_w, ff // NG), BF),
            dma((2, NF)),
            dma((4,)),
            dma((8, 3)),
            dma((32,)),
            dma((2,)),
            dma((4,)),
            dma((3,)),
            dma((4,)),
            dma((2,)),
            dma((2,)),
            dma((4, 2)),
            dma((2, 4)),
            dma((6, NF)),
            dma((6, NF)),
            dma((5, 4)),
            dma((5, 4)),
            dma((4, 2)),
            dma((8,)),
            dma((16,)),
            dma((16,)),
            dma((2, 2, NF)),
            dma((2, 2)),
            dma((2, 2)),
        ],
        compiler_params=pltpu.CompilerParams(
            collective_id=0, has_side_effects=True, vmem_limit_bytes=int(38.75 * 2**20)
        ),
        cost_estimate=pl.CostEstimate(
            flops=6 * rows * half * ff, bytes_accessed=4 * half * ff, transcendentals=rows * ff
        ),
    )(tokens, cotangent, expert_ids.T, route_weight.T, w_up, w_down)

    gb = 256
    gu, gd = pl.pallas_call(
        finish,
        grid=(half // gb,),
        out_shape=(grad, grad),
        in_specs=[
            pl.BlockSpec((gb, ff), lambda i: (i, 0)),
            pl.BlockSpec((gb, ff), lambda i: (i, 0)),
            pl.BlockSpec((2, FIN, gb), lambda i: (0, 0, i)),
            pl.BlockSpec((2, FIN, ff), lambda i: (0, 0, 0)),
        ],
        out_specs=(pl.BlockSpec((gb, ff), lambda i: (i, 0)),) * 2,
        compiler_params=pltpu.CompilerParams(vmem_limit_bytes=24 * 2**20),
    )(gu, gd, xd, ad)
    return out, gu[None], gd[None]


def solution(mesh):
    placed = (
        P(("dp", "expert"), None),
        P(("dp", "expert", "tensor"), None),
        P(("dp", "expert"), None),
        P(("dp", "expert"), None),
        P("expert", "dp", "tensor"),
        P("expert", "dp", "tensor"),
    )
    return jax.shard_map(
        shards,
        mesh=mesh,
        in_specs=placed,
        out_specs=(
            P(("dp", "expert", "tensor"), None),
            P("expert", "dp", "tensor"),
            P("expert", "dp", "tensor"),
        ),
        check_vma=False,
    )
```

time: 164 us -> 156 us (0.951)
  matrix products: 13 us -> 0 us
  Pallas kernels: 148 us -> 151 us
  local copies, waits for them, and re-layouts: 1.3 us -> 4.02 us
    dot_general x2 -> x0, matrix products: 13 us -> none  [grad(): lax.dot_general(left, right, (((0,), (0,)), ((), ())), preferred_element_...]
    pallas_call x0 -> x1, Pallas kernels: none -> 6.12 us  [shards(): pl.pallas_call(finish, grid=(half // gb,), out_shape=(grad, grad), in_spe...]
    unnamed x7 -> x9, local copies, waits for them, and re-layouts: 1.3 us -> 4.02 us
    pallas_call x1, Pallas kernels: 148 us -> 145 us  [shards(): pl.pallas_call(kernel, out_shape=(jax.ShapeDtypeStruct(cotangent.shape, B...]
where the time goes in v3:
time: 156 us
  Pallas kernels  151 us (97%)
  local copies, waits for them, and re-layouts  4.02 us (3%)
    pallas_call x1, Pallas kernels, shards(): pl.pallas_call(kernel, out_shape=(jax.ShapeDtypeStruct(cotangent.shape, B...  145 us
    pallas_call x1, Pallas kernels, shards(): pl.pallas_call(finish, grid=(half // gb,), out_shape=(grad, grad), in_spe...  6.12 us
    unnamed x9, local copies, waits for them, and re-layouts  4.02 us

profile of v3, /device:TPU:9, one launch (start us, length us, event | category | flops | bytes accessed | tf_op | source)
XLA Modules:
  0.0 155.9 jit_solution(9332837431744799707)
XLA Ops:
  0.6 0.0 copy-start
  0.6 1.1 copy-done
  1.8 0.0 copy-start.1
  1.8 0.9 copy-done.1
  2.7 0.0 copy-start.2
  2.7 0.7 copy-done.2
  3.3 0.0 copy-start.3
  3.3 0.7 copy-done.3
  4.0 145.1 %shard_map.85 = (bf16[16,3072]{1,0:T(8,128)(2,1)S(1)}, bf16[2,160,1536]{2,1,0:T(8,128)(2,1)S(1)}, bf16[2,160,2048]{2,1,0:T(8,128)(2,1)S(1)}, bf16[1536,2048]{1,0:T(8,128)(2,1)S(1)}, bf16[1536,2048]{1,0:T(8,128)(2,1)S(1)}) custom-call(bf16[128,3072]{1,0:T(8,128)(2,1)S(1)} %copy-done, bf16[16,3072]{1,0:T(8,128)(2,1)S(1)} %copy-done.1, s32[2,128]{1,0:T(2,128)S(1)} %bitcast.4, ...), custom_call_target="tpu_custom_call" | custom-call | flops 10871635968 | bytes 12582912 | tf_op jit(solution)/shard_map/pallas_call | solution.py:593
  149.2 6.1 %shard_map.86 = (bf16[1536,2048]{1,0:T(8,128)(2,1)}, bf16[1536,2048]{1,0:T(8,128)(2,1)}) custom-call(bf16[1536,2048]{1,0:T(8,128)(2,1)S(1)} %get-tuple-element.11.up_part, bf16[1536,2048]{1,0:T(8,128)(2,1)S(1)} %get-tuple-element.12.down_part, bf16[2,160,1536]{2,1,0:T(8,128)(2,1)S(1)} %get-tuple-element.13.xd, bf16[2,160,2048]{2,1,0:T(8,128)(2,1)S(1)} %get-tuple-element.14.ad), custom_call_target="tpu_custom_call" | custom-call | tf_op jit(solution)/shard_map/pallas_call | solution.py:659
  155.3 0.6 copy.10
Async XLA Ops:
  0.6 1.1 copy-start
  1.8 0.9 copy-start.1
  2.7 0.7 copy-start.2
  3.3 0.7 copy-start.3

commit v4 on v3

--- a/solution.py
+++ b/solution.py
@@ -496,11 +496,11 @@
         if k == 2:
             ad[0, :, LATE[0] :] = jnp.zeros((2, LATE[1], NF * fc), BF)
             gradients(0, 0, 4)
-            gradients(1, 0, 2)
+            gradients(1, 0, 1)
         if k == 3:
             absorb(5)
             spread(4)
-            gradients(1, 2, 3)
+            gradients(1, 1, 2)
         total = collect(k)
         give_back(k, 0, total[0 : 2 * CAP])
         if k == 0:
@@ -509,6 +509,7 @@
             give_back(k, 1, total[2 * CAP :])
 
     give_back(0, 1, jnp.concatenate([held[...], collect(4)], axis=0))
+    gradients(1, 2, 3)
 
     def res_wait(j):
         i = (e + j) % 8
@@ -655,7 +656,7 @@
         ),
     )(tokens, cotangent, expert_ids.T, route_weight.T, w_up, w_down)
 
-    gb = 256
+    gb = 384
     gu, gd = pl.pallas_call(
         finish,
         grid=(half // gb,),

time: 156 us -> 154 us (0.987)
  Pallas kernels: 151 us -> 149 us
    pallas_call x1, Pallas kernels: 145 us -> 143 us  [shards(): pl.pallas_call(kernel, out_shape=(jax.ShapeDtypeStruct(cotangent.shape, B...]
where the time goes in v4:
time: 154 us
  Pallas kernels  149 us (97%)
  local copies, waits for them, and re-layouts  4.02 us (3%)
    pallas_call x1, Pallas kernels, shards(): pl.pallas_call(kernel, out_shape=(jax.ShapeDtypeStruct(cotangent.shape, B...  143 us
    pallas_call x1, Pallas kernels, shards(): pl.pallas_call(finish, grid=(half // gb,), out_shape=(grad, grad), in_spe...  5.65 us
    unnamed x9, local copies, waits for them, and re-layouts  4.02 us

profile of v4, /device:TPU:9, one launch (start us, length us, event | category | flops | bytes accessed | tf_op | source)
XLA Modules:
  0.0 153.7 jit_solution(7302925777706897518)
XLA Ops:
  0.6 0.0 copy-start
  0.6 1.1 copy-done
  1.8 0.0 copy-start.1
  1.8 0.9 copy-done.1
  2.7 0.0 copy-start.2
  2.7 0.7 copy-done.2
  3.3 0.0 copy-start.3
  3.3 0.7 copy-done.3
  4.0 143.4 %shard_map.85 = (bf16[16,3072]{1,0:T(8,128)(2,1)S(1)}, bf16[2,160,1536]{2,1,0:T(8,128)(2,1)S(1)}, bf16[2,160,2048]{2,1,0:T(8,128)(2,1)S(1)}, bf16[1536,2048]{1,0:T(8,128)(2,1)S(1)}, bf16[1536,2048]{1,0:T(8,128)(2,1)S(1)}) custom-call(bf16[128,3072]{1,0:T(8,128)(2,1)S(1)} %copy-done, bf16[16,3072]{1,0:T(8,128)(2,1)S(1)} %copy-done.1, s32[2,128]{1,0:T(2,128)S(1)} %bitcast.4, ...), custom_call_target="tpu_custom_call" | custom-call | flops 10871635968 | bytes 12582912 | tf_op jit(solution)/shard_map/pallas_call | solution.py:594
  147.4 5.6 %shard_map.86 = (bf16[1536,2048]{1,0:T(8,128)(2,1)}, bf16[1536,2048]{1,0:T(8,128)(2,1)}) custom-call(bf16[1536,2048]{1,0:T(8,128)(2,1)S(1)} %get-tuple-element.11.up_part, bf16[1536,2048]{1,0:T(8,128)(2,1)S(1)} %get-tuple-element.12.down_part, bf16[2,160,1536]{2,1,0:T(8,128)(2,1)S(1)} %get-tuple-element.13.xd, bf16[2,160,2048]{2,1,0:T(8,128)(2,1)S(1)} %get-tuple-element.14.ad), custom_call_target="tpu_custom_call" | custom-call | tf_op jit(solution)/shard_map/pallas_call | solution.py:660
  153.1 0.6 copy.10
Async XLA Ops:
  0.6 1.1 copy-start
  1.8 0.9 copy-start.1
  2.7 0.7 copy-start.2
  3.3 0.7 copy-start.3

commit v5 on v4

--- a/solution.py
+++ b/solution.py
@@ -500,7 +500,6 @@
         if k == 3:
             absorb(5)
             spread(4)
-            gradients(1, 1, 2)
         total = collect(k)
         give_back(k, 0, total[0 : 2 * CAP])
         if k == 0:
@@ -508,6 +507,7 @@
         else:
             give_back(k, 1, total[2 * CAP :])
 
+    gradients(1, 1, 2)
     give_back(0, 1, jnp.concatenate([held[...], collect(4)], axis=0))
     gradients(1, 2, 3)
 
@@ -656,7 +656,7 @@
         ),
     )(tokens, cotangent, expert_ids.T, route_weight.T, w_up, w_down)
 
-    gb = 384
+    gb = 512
     gu, gd = pl.pallas_call(
         finish,
         grid=(half // gb,),

time: 154 us -> 154 us (level)
  no operation moved by 1% of the time
where the time goes in v5:
time: 154 us; the launch traced here: 153 us
  Pallas kernels  149 us (97%)
  local copies, waits for them, and re-layouts  4.02 us (3%)
    pallas_call x1, Pallas kernels, shards(): pl.pallas_call(kernel, out_shape=(jax.ShapeDtypeStruct(cotangent.shape, B...  143 us
    pallas_call x1, Pallas kernels, shards(): pl.pallas_call(finish, grid=(half // gb,), out_shape=(grad, grad), in_spe...  5.58 us
    unnamed x9, local copies, waits for them, and re-layouts  4.02 us

profile of v5, /device:TPU:9, one launch (start us, length us, event | category | flops | bytes accessed | tf_op | source)
XLA Modules:
  0.0 153.4 jit_solution(8468090201175660327)
XLA Ops:
  0.6 0.0 copy-start
  0.6 1.1 copy-done
  1.8 0.0 copy-start.1
  1.8 0.9 copy-done.1
  2.7 0.0 copy-start.2
  2.7 0.7 copy-done.2
  3.3 0.0 copy-start.3
  3.3 0.7 copy-done.3
  4.0 143.1 %shard_map.85 = (bf16[16,3072]{1,0:T(8,128)(2,1)S(1)}, bf16[2,160,1536]{2,1,0:T(8,128)(2,1)S(1)}, bf16[2,160,2048]{2,1,0:T(8,128)(2,1)S(1)}, bf16[1536,2048]{1,0:T(8,128)(2,1)S(1)}, bf16[1536,2048]{1,0:T(8,128)(2,1)S(1)}) custom-call(bf16[128,3072]{1,0:T(8,128)(2,1)S(1)} %copy-done, bf16[16,3072]{1,0:T(8,128)(2,1)S(1)} %copy-done.1, s32[2,128]{1,0:T(2,128)S(1)} %bitcast.4, ...), custom_call_target="tpu_custom_call" | custom-call | flops 10871635968 | bytes 12582912 | tf_op jit(solution)/shard_map/pallas_call | solution.py:594
  147.2 5.6 %shard_map.86 = (bf16[1536,2048]{1,0:T(8,128)(2,1)}, bf16[1536,2048]{1,0:T(8,128)(2,1)}) custom-call(bf16[1536,2048]{1,0:T(8,128)(2,1)S(1)} %get-tuple-element.11.up_part, bf16[1536,2048]{1,0:T(8,128)(2,1)S(1)} %get-tuple-element.12.down_part, bf16[2,160,1536]{2,1,0:T(8,128)(2,1)S(1)} %get-tuple-element.13.xd, bf16[2,160,2048]{2,1,0:T(8,128)(2,1)S(1)} %get-tuple-element.14.ad), custom_call_target="tpu_custom_call" | custom-call | tf_op jit(solution)/shard_map/pallas_call | solution.py:660
  152.7 0.6 copy.10
Async XLA Ops:
  0.6 1.1 copy-start
  1.8 0.9 copy-start.1
  2.7 0.7 copy-start.2
  3.3 0.7 copy-start.3
